TPU v7x, 32 devices: a whole 2x2x4 slice. The times are simulated.
32 devices in a mesh: dp: 4 (over y, core), seq: 8 (over z, x).
Axes of the slice: x: 2, y: 2, z: 4, core: 2. Of those that a mesh axis runs over, the one named last changes fastest.
Arguments:
- grad_out: bfloat16 [4, 1024, 4096], P('dp', 'seq'), may hold values from -6 to 6
- block_in: bfloat16 [4, 1024, 4096], P('dp', 'seq'), may hold values from -0.125 to 0.125
- residues: float32 [8, 4096], replicated, may hold values from -2 to 2
- decay_rates: float32 [8], replicated
Outputs:
- grad_in: bfloat16 [4, 1024, 4096], P('dp', 'seq')
- residue_grad: float32 [8, 4096], P(None, 'dp')
All inputs are finite; a program needn't handle non-finite values.
Results may differ from a plain program's by a relative error of at most 0.0068.
Values sent between devices are 32-bit elements; how exact they have to be, the bound alone decides.
No kernel may reach another device: no remote copies, remote signals or barrier semaphores. Data moves between devices by JAX's collectives and lax.ppermute only.
A program may use at most 64 MiB of HBM per device.

v0:
```python
import jax
import jax.numpy as jnp
from jax import lax
from jax.sharding import PartitionSpec as P


def prefix(shard, axis, combine, identity):
    count, index = (lax.axis_size(axis), lax.axis_index(axis))
    everything = jax.tree.map(lambda part: lax.all_gather(part, axis), shard)
    start = jax.tree.map(
        lambda part, zero: jnp.broadcast_to(jnp.asarray(zero, part.dtype), part.shape),
        shard,
        identity,
    )

    def step(k, before):
        at = count - 1 - k
        reached = at > index
        new = combine(before, jax.tree.map(lambda part: part[at], everything))
        return jax.tree.map(lambda a, b: jnp.where(reached, a, b), new, before)

    return lax.fori_loop(0, count, step, start)


def modal_tables(decay_rates, block_rows):
    offsets = jnp.arange(block_rows, dtype=jnp.float32)
    mode_gain = jnp.sqrt(1.0 - jnp.exp(-2.0 * decay_rates))
    lag_steps = offsets[None, :] - offsets[:, None]
    decay_table = jnp.where(
        lag_steps[None] >= 0,
        mode_gain[:, None, None]
        * jnp.exp(-decay_rates[:, None, None] * jnp.maximum(lag_steps[None], 0.0)),
        0.0,
    ).astype(jnp.bfloat16)
    carry_table = (
        mode_gain[None, :] * jnp.exp(-decay_rates[None, :] * (block_rows - offsets[:, None]))
    ).astype(jnp.bfloat16)
    state_table = jnp.exp(-decay_rates[:, None] * offsets[None, :]).astype(jnp.bfloat16)
    block_decay = jnp.exp(-decay_rates * block_rows)
    return (decay_table, carry_table, state_table, block_decay)


def local_terms(grad_out, block_in, residues, decay_table, carry_table, state_table):
    batch_rows, block_rows, channel_count = grad_out.shape
    mode_count = residues.shape[0]
    stacked_table = jnp.transpose(decay_table, (1, 0, 2)).reshape(
        block_rows, mode_count * block_rows
    )
    scaled = (
        (grad_out[:, None, :, :] * residues[None, :, None, :])
        .astype(jnp.bfloat16)
        .reshape(batch_rows, mode_count * block_rows, channel_count)
    )
    local_grad = jnp.einsum(
        "sk,bkc->bsc", stacked_table, scaled, preferred_element_type=jnp.float32
    )
    block_state = jnp.einsum(
        "rt,btc->brc", state_table, grad_out, preferred_element_type=jnp.float32
    )
    pieces = []
    for mode_index in range(mode_count):
        weighted = jnp.einsum(
            "st,bsc->btc", decay_table[mode_index], block_in, preferred_element_type=jnp.float32
        )
        pieces.append(jnp.sum(weighted * grad_out, axis=(0, 1)))
    local_part = jnp.stack(pieces)
    carry_weights = jnp.einsum(
        "sr,bsc->brc", carry_table, block_in, preferred_element_type=jnp.float32
    )
    return (local_grad, block_state, local_part, carry_weights)


def local(grad_out, block_in, residues, decay_rates):
    batch_rows, block_rows, channel_count = grad_out.shape
    decay_table, carry_table, state_table, block_decay = modal_tables(decay_rates, block_rows)
    local_grad, block_state, local_part, carry_weights = local_terms(
        grad_out, block_in, residues, decay_table, carry_table, state_table
    )
    decay_stack = block_decay[None, :, None]

    def combine(earlier_part, later_part):
        return (later_part[0] * earlier_part[0], later_part[1] + later_part[0] * earlier_part[1])

    identity = (jnp.ones_like(decay_stack), jnp.zeros_like(block_state))
    incoming = prefix((decay_stack, block_state), "seq", combine, identity)[1]
    carried = jnp.einsum(
        "sr,brc->bsc",
        carry_table.astype(jnp.float32),
        residues[None] * incoming,
        precision=lax.Precision.HIGHEST,
    )
    grad_in = (local_grad + carried).astype(jnp.bfloat16)
    partial_value = local_part + jnp.sum(incoming * carry_weights, axis=0)
    whole_sum = lax.psum(partial_value, "seq")
    residue_grad = lax.psum_scatter(whole_sum, "dp", scatter_dimension=1, tiled=True)
    return (grad_in, residue_grad)


def solution(mesh):
    placed = (P("dp", "seq", None), P("dp", "seq", None), P(), P())
    return jax.shard_map(
        local,
        mesh=mesh,
        in_specs=placed,
        out_specs=(P("dp", "seq", None), P(None, "dp")),
        check_vma=False,
    )
```

profile of v0, /device:TPU:0, one launch (start us, length us, event | category | flops | bytes accessed | tf_op | source)
XLA Modules:
  0.0 133.8 jit_solution(10111617546309197878)
XLA Ops:
  7.2 1.3 dynamic-slice
  10.0 2.2 %convolution_bitcast_fusion.9 = f32[1,8,4096]{2,1,0:T(8,128)} fusion(bf16[1,128,4096]{2,1,0:T(8,128)(2,1)} %param.6, f32[8]{0:T(128)S(1)} %get-tuple-element.178), kind=kOutput, calls=%fused_computation.28 | convolution fusion | flops 8390656 | bytes 1179680 | tf_op jit(solution)/shard_map/rt,btc->brc/dot_general | solution.py:57
  12.2 2.7 %bitcast_convert_fusion = f32[128,4096]{1,0:T(8,128)} fusion(bf16[1,128,4096]{2,1,0:T(8,128)(2,1)} %param.6), kind=kLoop, calls=%fused_computation.50 | loop fusion | flops 524288 | bytes 3145728 | tf_op jit(solution)/shard_map/convert_element_type | solution.py:50
  15.1 3.0 %copy.10 = f32[128,4096]{0,1:T(8,128)} copy(f32[128,4096]{1,0:T(8,128)} %bitcast_convert_fusion) | data formatting | bytes 4194304 | tf_op jit(solution)/shard_map/convert_element_type | solution.py:50
  18.1 23.1 %all-reduce = f32[64]{0:T(128)S(1)} all-reduce(f32[64]{0:T(128)S(1)} %get-tuple-element.177), channel_id=3, replica_groups=mesh['dp'=4,'seq'=8] {'seq'}, use_global_device_ids=true, to_apply=%add | all-reduce | flops 64 | bytes 512
  44.5 1.1 fusion.15
  45.5 1.1 fusion.16
  46.6 1.1 fusion.17
  47.7 1.1 stack.35
  48.8 6.4 %all-gather.4.cloned.1.call-done = f32[8,8,4096]{2,1,0:T(8,128)} async-done(((f32[1,8,4096]{2,1,0:T(8,128)}), f32[8,8,4096]{2,1,0:T(8,128)}) %all-gather.4.cloned.1.call-update) | async-done | bytes 1048592 | tf_op jit(solution)/shard_map/all_gather | solution.py:9
  55.2 13.2 %while.16 = (s32[]{:T(128)}, f32[1,8,4096]{2,1,0:T(8,128)S(1)}, s32[]{:T(128)}, f32[8,1,8,4096]{3,2,1,0:T(8,128)}, f32[8,1,8,1]{2,3,1,0:T(1,128)}, /*index=5*/s32[]{:T(128)}, s32[]{:T(128)}, s32[]{:T(128)}, s32[]{:T(128)}) while((s32[]{:T(128)}, f32[1,8,4096]{2,1,0:T(8,128)S(1)}, s32[]{:T(128)}, f32[8,1,8,4096]{3,2,1,0:T(8,128)}, ...), condition=%wide.region_1.2_spmd.clone, body=%wide.region_0.1_spmd.clone.sunk | while | flops 131080 | bytes 393487 | solution.py:22
  55.9 1.0 fusion.45
  57.6 1.0 fusion.45
  59.2 1.0 fusion.45
  60.9 1.0 fusion.45
  62.6 1.0 fusion.45
  64.2 1.0 fusion.45
  65.8 1.0 fusion.45
  68.4 1.7 %fusion.9 = f32[8,4096]{1,0:T(8,128)} fusion(f32[8,4096]{1,0:T(8,128)S(1)} %stack.35, f32[1,8,4096]{2,1,0:T(8,128)S(1)} %get-tuple-element.134, bf16[1,128,4096]{2,1,0:T(8,128)(2,1)S(1)} %copy-done, f32[128]{0:T(128)S(1)} %iota_subtract_fusion.1, f32[8]{0:T(128)} %copy-done.6, f32[8]{0:T(128)} %copy-done.8), kind=kOutput, calls=%fused_computation.31 | convolution fusion | flops 8457216 | bytes 1442368 | tf_op jit(solution)/shard_map/sr,bsc->brc/dot_general | solution.py:67
  70.2 5.5 %fusion.4 = f32[4096,128]{1,0:T(8,128)S(1)} fusion(f32[8,4096]{1,0:T(8,128)} %param.8, f32[128,4096]{0,1:T(8,128)S(1)} %copy-done.2, f32[128,128]{1,0:T(8,128)S(1)} %fusion.34, f32[8]{0:T(128)S(1)} %copy-done.7, f32[8]{0:T(128)S(1)} %copy-done.9, pred[128,128]{1,0:T(8,128)(4,1)S(1)} %copy-done.5), kind=kOutput, calls=%fused_computation.15 | convolution fusion | flops 1082654720 | bytes 4407360 | tf_op jit(solution)/shard_map/sk,bkc->bsc/dot_general | solution.py:54
  75.8 1.8 %fusion.6 = bf16[1,128,4096]{1,2,0:T(8,128)(2,1)S(1)} fusion(f32[4096,128]{1,0:T(8,128)S(1)} %fusion.4, f32[1,8,4096]{2,1,0:T(8,128)S(1)} %get-tuple-element.134, f32[8,4096]{1,0:T(8,128)S(1)} %copy-done.3, f32[128]{0:T(128)S(1)} %iota_subtract_fusion.1, f32[8]{0:T(128)S(1)} %copy-done.7, f32[8]{0:T(128)S(1)} %copy-done.9), kind=kOutput, calls=%fused_computation.26 | convolution fusion | flops 51416064 | bytes 3408448 | tf_op jit(solution)/shard_map/sr,brc->bsc/dot_general | solution.py:86
  77.6 1.3 copy.13
  78.9 9.7 %reduce-scatter.2.cloned.1.call-done = f32[8,1024]{1,0:T(8,128)} async-done(((f32[8,4096]{1,0:T(8,128)}), f32[8,1024]{1,0:T(8,128)}) %reduce-scatter.2.cloned.1.call-update) | async-done | bytes 32784 | tf_op jit(solution)/shard_map/reduce_scatter | solution.py:95
  88.6 38.3 %psum.8 = f32[8,1024]{1,0:T(8,128)} all-reduce(f32[8,1024]{1,0:T(8,128)} %reduce-scatter.2.cloned.1.call-done), channel_id=1, replica_groups=mesh['dp'=4,'seq'=8] {'seq'}, use_global_device_ids=true, to_apply=%region_10.11 | all-reduce | flops 8192 | bytes 65536 | tf_op jit(solution)/shard_map/psum | solution.py:94
  (46 shorter events, 10.3 us)
Async XLA Ops:
  7.2 34.9 %copy-start = (bf16[1,128,4096]{2,1,0:T(8,128)(2,1)S(1)}, bf16[1,128,4096]{2,1,0:T(8,128)(2,1)}, u32[]{:S(2)}) copy-start(bf16[1,128,4096]{2,1,0:T(8,128)(2,1)} %param.7) | copy-start | bytes 3145732
  7.2 48.1 %all-gather.4.cloned.1.call-start = ((), (), s32[]{:S(2)}) async-start(), calls=%async_computation.1 | async-start | bytes 1179648 | tf_op jit(solution)/shard_map/all_gather | solution.py:9
  10.0 31.9 %copy-start.6 = (f32[8]{0:T(128)}, f32[8]{0:T(128)S(1)}, u32[]{:S(2)}) copy-start(f32[8]{0:T(128)S(1)} %get-tuple-element.178) | copy-start | bytes 100
  10.0 31.9 %copy-start.8 = (f32[8]{0:T(128)}, f32[8]{0:T(128)S(1)}, u32[]{:S(2)}) copy-start(f32[8]{0:T(128)S(1)} %get-tuple-element.179) | copy-start | bytes 100
  12.2 76.4 %reduce-scatter.2.cloned.1.call-start = ((), (), s32[]{:S(2)}) async-start(), calls=%async_computation.2 | async-start | bytes 163840 | tf_op jit(solution)/shard_map/reduce_scatter | solution.py:95
  15.0 26.8 %copy-start.4 = (pred[128,128]{1,0:T(8,128)(4,1)}, pred[128,128]{1,0:T(8,128)(4,1)S(1)}, u32[]{:S(2)}) copy-start(pred[128,128]{1,0:T(8,128)(4,1)S(1)} %fusion.35) | copy-start | bytes 49156
  15.1 27.0 %copy-start.1 = (bf16[1,128,4096]{2,1,0:T(8,128)(2,1)S(1)}, bf16[1,128,4096]{2,1,0:T(8,128)(2,1)}, u32[]{:S(2)}) copy-start(bf16[1,128,4096]{2,1,0:T(8,128)(2,1)} %param.6) | copy-start | bytes 3145732
  47.7 22.5 %copy-start.2 = (f32[128,4096]{0,1:T(8,128)S(1)}, f32[128,4096]{0,1:T(8,128)}, u32[]{:S(2)}) copy-start(f32[128,4096]{0,1:T(8,128)} %copy.10) | copy-start | bytes 6291460
  48.8 21.4 %copy-start.5 = (pred[128,128]{1,0:T(8,128)(4,1)S(1)}, pred[128,128]{1,0:T(8,128)(4,1)}, u32[]{:S(2)}) copy-start(pred[128,128]{1,0:T(8,128)(4,1)} %copy-done.4) | copy-start | bytes 49156
  48.8 21.4 %copy-start.7 = (f32[8]{0:T(128)S(1)}, f32[8]{0:T(128)}, u32[]{:S(2)}) copy-start(f32[8]{0:T(128)} %copy-done.6) | copy-start | bytes 100
  48.8 21.4 %copy-start.9 = (f32[8]{0:T(128)S(1)}, f32[8]{0:T(128)}, u32[]{:S(2)}) copy-start(f32[8]{0:T(128)} %copy-done.8) | copy-start | bytes 100
  70.2 5.6 %copy-start.3 = (f32[8,4096]{1,0:T(8,128)S(1)}, f32[8,4096]{1,0:T(8,128)}, u32[]{:S(2)}) copy-start(f32[8,4096]{1,0:T(8,128)} %param.8) | copy-start | bytes 393220
Sparse Core Ops, SparseCore 0:
  12.3 42.8 all-gather.3
  70.3 18.3 reduce-scatter.1
where the time goes:
time: 134 us
  blocking collectives  61.4 us (46%)
  matrix products  16.9 us (13%)
  waiting for transfers between devices  16.2 us (12%)
  between operations  14.9 us (11%)
  local copies, waits for them, and re-layouts  12.6 us (9%)
  other arithmetic  11.6 us (9%)
    psum x1, blocking collectives, local(): whole_sum = lax.psum(partial_value, 'seq')  38.3 us
    unnamed x1, blocking collectives  23.1 us
    reduce_scatter x1, waiting for transfers between devices, local(): lax.psum_scatter(whole_sum, 'dp', scatter_dimension=1, tiled=True)  9.71 us
    select_n x8, other arithmetic, step(): return jax.tree.map(lambda a, b: jnp.where(reached, a, b), new, before)  7.91 us
    all_gather x1, waiting for transfers between devices, prefix(): everything = jax.tree.map(lambda part: lax.all_gather(part, axis), shard)  6.42 us
    dot_general x8, matrix products, local_terms(): jnp.einsum('st,bsc->btc', decay_table[mode_index], block_in, preferred_el...  5.56 us
    dot_general x1, matrix products, local_terms(): jnp.einsum('sk,bkc->bsc', stacked_table, scaled, preferred_element_type=j...  5.54 us
    mul x8, local copies, waits for them, and re-layouts, combine(): later_part[0] * earlier_part[1]  5.08 us
  transfers between devices with their start and end apart: 2, of which 2 were waited for; matrix products, arithmetic and copies ran while one was open for 16% of the time, Pallas kernels for 0%

commit v1 on v0

v1 whole, which is shorter than its diff:
```python
import functools

import jax
import jax.numpy as jnp
from jax import lax
from jax.experimental import pallas as pl
from jax.experimental.pallas import tpu as pltpu
from jax.sharding import PartitionSpec as P

VMEM_LIMIT = 48 * 1024 * 1024
LANES = 128


def rate_column(rates_ref, mode_count, width):
    rows = lax.broadcasted_iota(jnp.int32, (mode_count, width), 0)
    column = jnp.zeros((mode_count, width), jnp.float32)
    for r in range(mode_count):
        column = jnp.where(rows == r, rates_ref[r], column)
    return column


def mode_gain(rates):
    return jnp.sqrt(1.0 - jnp.exp(-2.0 * rates))


def decay_matrix(rate, rows, earlier_first):
    down = lax.broadcasted_iota(jnp.int32, (rows, rows), 0)
    across = lax.broadcasted_iota(jnp.int32, (rows, rows), 1)
    lag = (across - down if earlier_first else down - across).astype(jnp.float32)
    rates = jnp.full((rows, rows), rate, jnp.float32)
    gain = mode_gain(jnp.full((8, rows), rate, jnp.float32))[:1]
    table = gain * jnp.exp(-rates * jnp.maximum(lag, 0.0))
    return jnp.where(lag >= 0.0, table, 0.0).astype(jnp.bfloat16)


def terms_kernel(sub, rates_ref, grad_ref, in_ref, out_ref, decay_ref, pair_ref):
    mode_count = rates_ref.shape[0]
    rows, width = grad_ref.shape[1:]

    @pl.when(pl.program_id(0) == 0)
    def _():
        for r in range(mode_count):
            decay_ref[r * rows : (r + 1) * rows, :] = decay_matrix(rates_ref[r], rows, False)
        rates = rate_column(rates_ref, mode_count, rows)
        offset = lax.broadcasted_iota(jnp.int32, (mode_count, rows), 1).astype(jnp.float32)
        state = jnp.exp(-rates * offset)
        carry = mode_gain(rates) * jnp.exp(-rates * (rows - offset))
        pair_ref[...] = jnp.concatenate([state, carry], axis=0).astype(jnp.bfloat16)

    for first in range(0, width, sub):
        part = slice(first, first + sub)
        grad = grad_ref[0, :, part]
        block = in_ref[0, :, part]
        state = jnp.dot(pair_ref[...], grad, preferred_element_type=jnp.float32)[:mode_count]
        carry = jnp.dot(pair_ref[...], block, preferred_element_type=jnp.float32)[mode_count:]
        grad32 = grad.astype(jnp.float32)
        sums = []
        for r in range(mode_count):
            weighted = jnp.dot(
                decay_ref[r * rows : (r + 1) * rows, :], block, preferred_element_type=jnp.float32
            )
            sums.append(jnp.sum(weighted * grad32, axis=0, keepdims=True))
        local = jnp.concatenate(sums, axis=0)
        for k in range(sub // LANES):
            lanes = slice(k * LANES, (k + 1) * LANES)
            chunk = first // LANES + k
            out_ref[chunk, 0:mode_count, :] = state[:, lanes]
            out_ref[chunk, mode_count : 2 * mode_count, :] = carry[:, lanes]
            out_ref[chunk, 2 * mode_count : 3 * mode_count, :] = local[:, lanes]


def local_grad_kernel(sub, rates_ref, residues_ref, grad_ref, out_ref, decay_ref):
    mode_count = rates_ref.shape[0]
    rows, width = grad_ref.shape[1:]

    @pl.when(pl.program_id(0) == 0)
    def _():
        for r in range(mode_count):
            decay_ref[:, r * rows : (r + 1) * rows] = decay_matrix(rates_ref[r], rows, True)

    for first in range(0, width, sub):
        part = slice(first, first + sub)
        grad32 = grad_ref[0, :, part].astype(jnp.float32)
        scaled = jnp.concatenate(
            [
                (grad32 * residues_ref[r : r + 1, part]).astype(jnp.bfloat16)
                for r in range(mode_count)
            ],
            axis=0,
        )
        out_ref[:, part] = jnp.dot(decay_ref[...], scaled, preferred_element_type=jnp.float32)


def scan_kernel(batch_count, block_count, rates_ref, terms_ref, out_ref):
    mode_count = rates_ref.shape[0]
    width = terms_ref.shape[2]
    block_rows = LANES
    decay = jnp.exp(-rate_column(rates_ref, mode_count, width) * block_rows)
    zero = jnp.zeros((mode_count, width), jnp.float32)

    def sequence(b, total):
        def block(j, state):
            total, incoming = state
            at = (b + 1) * block_count - 1 - j
            out_ref[at, 0:mode_count, :] = incoming
            carry = terms_ref[at, mode_count : 2 * mode_count, :]
            total = total + (terms_ref[at, 2 * mode_count : 3 * mode_count, :] + incoming * carry)
            return total, terms_ref[at, 0:mode_count, :] + decay * incoming

        return lax.fori_loop(0, block_count, block, (total, zero), unroll=block_count <= 8)[0]

    total = lax.fori_loop(0, batch_count, sequence, zero, unroll=batch_count <= 8)

    def spread(at, carry):
        out_ref[at, mode_count : 2 * mode_count, :] = total
        return carry

    lax.fori_loop(0, batch_count * block_count, spread, 0, unroll=8)


def finish_kernel(rates_ref, residues_ref, local_ref, back_ref, grad_ref, sum_ref):
    mode_count = rates_ref.shape[0]
    rows, width = local_ref.shape
    step = pl.program_id(0)
    chunks = width // LANES
    rates = rate_column(rates_ref, mode_count, rows)
    offset = lax.broadcasted_iota(jnp.int32, (mode_count, rows), 1).astype(jnp.float32)
    carry = mode_gain(rates) * jnp.exp(-rates * (rows - offset))
    carry3 = jnp.concatenate([carry, carry, carry], axis=0).astype(jnp.bfloat16)
    pieces = []
    for k in range(chunks):
        lanes = slice(k * LANES, (k + 1) * LANES)
        rest = residues_ref[:, lanes] * back_ref[step * chunks + k, 0:mode_count, :]
        split = []
        for _ in range(3):
            split.append(rest.astype(jnp.bfloat16).astype(jnp.float32))
            rest = rest - split[-1]
        pieces.append(jnp.concatenate(split, axis=0).astype(jnp.bfloat16))
    carried = lax.dot_general(
        carry3,
        jnp.concatenate(pieces, axis=1),
        (((0,), (0,)), ((), ())),
        preferred_element_type=jnp.float32,
    )
    grad_ref[0] = (local_ref[...] + carried).astype(jnp.bfloat16)

    @pl.when(step == 0)
    def _():
        own = sum_ref.shape[1] // LANES
        base = lax.axis_index("dp") * own
        for k in range(own):
            sum_ref[:, k * LANES : (k + 1) * LANES] = back_ref[base + k, mode_count : 2 * mode_count, :]


def to_owners(chunks, owners):
    count, rows, lanes = chunks.shape
    if owners == count:
        return chunks
    narrow = count * lanes // owners
    parts = chunks.reshape(count, rows, lanes // narrow, narrow)
    return jnp.swapaxes(parts, 1, 2).reshape(owners, rows, narrow)


def from_owners(parts, count):
    owners, rows, narrow = parts.shape
    if owners == count:
        return parts
    chunks = parts.reshape(count, owners // count, rows, narrow)
    return jnp.swapaxes(chunks, 1, 2).reshape(count, rows, LANES)


def params():
    return pltpu.CompilerParams(vmem_limit_bytes=VMEM_LIMIT)


def local(batch_count, block_count, grad_out, block_in, residues, decay_rates):
    _, rows, channels = grad_out.shape
    modes = residues.shape[0]
    owners = batch_count * block_count
    smem = pl.BlockSpec(memory_space=pltpu.SMEM)
    width = 1024
    steps = channels // width
    rows_block = pl.BlockSpec((1, rows, width), lambda i: (0, 0, i))
    terms = pl.pallas_call(
        functools.partial(terms_kernel, 256),
        grid=(steps,),
        in_specs=[smem, rows_block, rows_block],
        out_specs=pl.BlockSpec((width // LANES, 3 * modes, LANES), lambda i: (i, 0, 0)),
        out_shape=jax.ShapeDtypeStruct((channels // LANES, 3 * modes, LANES), jnp.float32),
        scratch_shapes=[
            pltpu.VMEM((modes * rows, rows), jnp.bfloat16),
            pltpu.VMEM((2 * modes, rows), jnp.bfloat16),
        ],
        compiler_params=params(),
        name="terms",
    )(decay_rates, grad_out, block_in)
    terms = lax.all_to_all(to_owners(terms, owners), ("dp", "seq"), 0, 0)
    local_grad = pl.pallas_call(
        functools.partial(local_grad_kernel, 256),
        grid=(steps,),
        in_specs=[smem, pl.BlockSpec((modes, width), lambda i: (0, i)), rows_block],
        out_specs=pl.BlockSpec((rows, width), lambda i: (0, i)),
        out_shape=jax.ShapeDtypeStruct((rows, channels), jnp.float32),
        scratch_shapes=[pltpu.VMEM((rows, modes * rows), jnp.bfloat16)],
        compiler_params=params(),
        cost_estimate=pl.CostEstimate(
            flops=2 * rows * modes * rows * channels,
            bytes_accessed=6 * rows * channels,
            transcendentals=0,
        ),
        name="local_grad",
    )(decay_rates, residues, grad_out)
    whole = pl.BlockSpec(memory_space=pltpu.VMEM)
    back = pl.pallas_call(
        functools.partial(scan_kernel, batch_count, block_count),
        in_specs=[smem, whole],
        out_specs=whole,
        out_shape=jax.ShapeDtypeStruct((owners, 2 * modes, channels // owners), jnp.float32),
        compiler_params=params(),
        name="scan",
    )(decay_rates, terms)
    back = from_owners(lax.all_to_all(back, ("dp", "seq"), 0, 0), channels // LANES)
    return pl.pallas_call(
        finish_kernel,
        grid=(steps,),
        in_specs=[
            smem,
            pl.BlockSpec((modes, width), lambda i: (0, i)),
            pl.BlockSpec((rows, width), lambda i: (0, i)),
            pl.BlockSpec((channels // LANES, 2 * modes, LANES), lambda i: (0, 0, 0)),
        ],
        out_specs=[rows_block, pl.BlockSpec((modes, channels // batch_count), lambda i: (0, 0))],
        out_shape=[
            jax.ShapeDtypeStruct((1, rows, channels), jnp.bfloat16),
            jax.ShapeDtypeStruct((modes, channels // batch_count), jnp.float32),
        ],
        compiler_params=params(),
        name="finish",
    )(decay_rates, residues, local_grad, back)


def solution(mesh):
    placed = (P("dp", "seq", None), P("dp", "seq", None), P(), P())
    return jax.shard_map(
        functools.partial(local, mesh.shape["dp"], mesh.shape["seq"]),
        mesh=mesh,
        in_specs=placed,
        out_specs=(P("dp", "seq", None), P(None, "dp")),
        check_vma=False,
    )
```

time: 134 us -> 46.4 us (0.35)
  blocking collectives: 61.4 us -> 20.6 us
  matrix products: 16.9 us -> 0 us
  between operations: 14.9 us -> 0.69 us
  other arithmetic: 11.6 us -> 0 us
  Pallas kernels: 0 us -> 11.2 us
  local copies, waits for them, and re-layouts: 12.6 us -> 3.11 us
  waiting for transfers between devices: 16.2 us -> 7.81 us
  starting transfers between devices: 0.08 us -> 2.59 us
    psum x1 -> x0, blocking collectives: 38.3 us -> none  [local(): whole_sum = lax.psum(partial_value, 'seq')]
    unnamed x1 -> x0, blocking collectives: 23.1 us -> none
    all_to_all x0 -> x1, blocking collectives: none -> 20.6 us  [local(): terms = lax.all_to_all(to_owners(terms, owners), ('dp', 'seq'), 0, 0)]
    dot_general x12 -> x0, matrix products: 16.9 us -> none  [the longest x8 5.56 us: local_terms(): jnp.einsum('st,bsc->btc', decay_table[mode_index], block_in, preferred_el...]
    pallas_call x0 -> x4, Pallas kernels: none -> 11.2 us  [the longest x1 4.23 us: local(): pl.pallas_call(functools.partial(terms_kernel, 256), grid=(steps,), in_sp...]
    reduce_scatter x1 -> x0, waiting for transfers between devices: 9.71 us -> none  [local(): lax.psum_scatter(whole_sum, 'dp', scatter_dimension=1, tiled=True)]
    select_n x8 -> x0, other arithmetic: 7.91 us -> none  [step(): return jax.tree.map(lambda a, b: jnp.where(reached, a, b), new, before)]
    all_to_all x0 -> x1, waiting for transfers between devices: none -> 7.81 us  [local(): lax.all_to_all(back, ('dp', 'seq'), 0, 0)]
  transfers between devices with their start and end apart: 2 -> 1, of which waited for: 2 -> 1; matrix products, arithmetic and copies ran while one was open for 16% -> 0% of each run, Pallas kernels for 0% -> 6%
where the time goes in v1:
time: 46.4 us; the launch traced here: 46.1 us
  blocking collectives  20.6 us (44%)
  Pallas kernels  11.2 us (24%)
  waiting for transfers between devices  7.81 us (17%)
  local copies, waits for them, and re-layouts  3.11 us (7%)
  starting transfers between devices  2.59 us (6%)
  between operations  0.69 us (1%)
    all_to_all x1, blocking collectives, local(): terms = lax.all_to_all(to_owners(terms, owners), ('dp', 'seq'), 0, 0)  20.6 us
    all_to_all x1, waiting for transfers between devices, local(): lax.all_to_all(back, ('dp', 'seq'), 0, 0)  7.81 us
    pallas_call x1, Pallas kernels, local(): pl.pallas_call(functools.partial(terms_kernel, 256), grid=(steps,), in_sp...  4.23 us
    unnamed x12, local copies, waits for them, and re-layouts  3.11 us
    pallas_call x1, Pallas kernels, local(): pl.pallas_call(finish_kernel, grid=(steps,), in_specs=[smem, pl.BlockSpec...  2.9 us
    pallas_call x1, Pallas kernels, local(): pl.pallas_call(functools.partial(local_grad_kernel, 256), grid=(steps,),...  2.8 us
    all_to_all x1, starting transfers between devices, local(): lax.all_to_all(back, ('dp', 'seq'), 0, 0)  2.59 us
    pallas_call x1, Pallas kernels, local(): pl.pallas_call(functools.partial(scan_kernel, batch_count, block_count),...  1.31 us
  transfers between devices with their start and end apart: 1, of which 1 were waited for; matrix products, arithmetic and copies ran while one was open for 0% of the time, Pallas kernels for 6%

profile of v1, /device:TPU:0, one launch (start us, length us, event | category | flops | bytes accessed | tf_op | source)
XLA Modules:
  0.0 46.1 jit_solution(2768428184662741712)
XLA Ops:
  0.6 0.0 copy-start
  0.6 1.2 %copy-done = bf16[1,128,4096]{2,1,0:T(8,128)(2,1)S(1)} copy-done((bf16[1,128,4096]{2,1,0:T(8,128)(2,1)S(1)}, bf16[1,128,4096]{2,1,0:T(8,128)(2,1)}, u32[]{:S(2)}) %copy-start) | copy-done | bytes 1048600
  1.9 0.0 copy-start.1
  1.9 1.2 %copy-done.1 = bf16[1,128,4096]{2,1,0:T(8,128)(2,1)S(1)} copy-done((bf16[1,128,4096]{2,1,0:T(8,128)(2,1)S(1)}, bf16[1,128,4096]{2,1,0:T(8,128)(2,1)}, u32[]{:S(2)}) %copy-start.1) | copy-done | bytes 1048600
  3.1 0.0 copy-start.4
  3.1 0.7 %copy-done.4 = f32[8]{0:T(128)S(1)} copy-done((f32[8]{0:T(128)S(1)}, f32[8]{0:T(128)}, u32[]{:S(2)}) %copy-start.4) | copy-done | bytes 56
  3.7 0.0 copy-start.2
  3.7 0.0 copy-start.3
  3.7 0.0 copy-start.5
  3.7 4.2 %terms.1 = f32[32,24,128]{2,1,0:T(8,128)S(1)} custom-call(f32[8]{0:T(128)S(1)} %copy-done.4, bf16[1,128,4096]{2,1,0:T(8,128)(2,1)S(1)} %copy-done.1, bf16[1,128,4096]{2,1,0:T(8,128)(2,1)S(1)} %copy-done), custom_call_target="tpu_custom_call" | custom-call | tf_op jit(solution)/shard_map/terms/pallas_call | solution.py:184
  8.0 20.6 %all_to_all.10.terms_ref = f32[32,24,128]{2,1,0:T(8,128)S(1)} all-to-all(f32[32,24,128]{2,1,0:T(8,128)S(1)} %terms.1), channel_id=1, replica_groups=mesh['dp'=4,'seq'=8] {'dp','seq'}, dimensions={0} | all-to-all | bytes 786432 | tf_op jit(solution)/shard_map/all_to_all | solution.py:197
  28.6 1.3 %scan.1 = f32[32,16,128]{2,1,0:T(8,128)} custom-call(f32[8]{0:T(128)S(1)} %copy-done.4, f32[32,24,128]{2,1,0:T(8,128)S(1)} %all_to_all.10.terms_ref), custom_call_target="tpu_custom_call" | custom-call | tf_op jit(solution)/shard_map/scan/pallas_call | solution.py:214
  29.9 2.6 %all-to-all-start.1 = ((f32[32,16,128]{2,1,0:T(8,128)}), f32[32,16,128]{2,1,0:T(8,128)S(1)}, u32[]{:S(2)}, u32[]{:S(2)}) async-start(f32[32,16,128]{2,1,0:T(8,128)} %scan.1), calls=%async_computation.1 | async-start | bytes 524288 | tf_op jit(solution)/shard_map/all_to_all | solution.py:222
  32.5 0.0 copy-done.2
  32.5 0.0 copy-done.3
  32.6 0.0 copy-done.5
  32.6 2.8 %local_grad.1.local_ref = f32[128,4096]{1,0:T(8,128)S(1)} custom-call(f32[8]{0:T(128)S(1)} %copy-done.5, f32[8,4096]{1,0:T(8,128)S(1)} %copy-done.3, bf16[1,128,4096]{2,1,0:T(8,128)(2,1)S(1)} %copy-done.2), custom_call_target="tpu_custom_call" | custom-call | flops 1073741824 | bytes 3145728 | tf_op jit(solution)/shard_map/local_grad/pallas_call | solution.py:198
  35.4 7.8 %all-to-all-done.1.back_ref = f32[32,16,128]{2,1,0:T(8,128)S(1)} async-done(((f32[32,16,128]{2,1,0:T(8,128)}), f32[32,16,128]{2,1,0:T(8,128)S(1)}, u32[]{:S(2)}, u32[]{:S(2)}) %all-to-all-start.1) | async-done | bytes 262176 | tf_op jit(solution)/shard_map/all_to_all | solution.py:222
  43.2 2.9 %finish.1 = (bf16[1,128,4096]{2,1,0:T(8,128)(2,1)}, f32[8,1024]{1,0:T(8,128)}) custom-call(f32[8]{0:T(128)S(1)} %copy-done.5, f32[8,4096]{1,0:T(8,128)S(1)} %copy-done.3, f32[128,4096]{1,0:T(8,128)S(1)} %local_grad.1.local_ref, f32[32,16,128]{2,1,0:T(8,128)S(1)} %all-to-all-done.1.back_ref), custom_call_target="tpu_custom_call" | custom-call | tf_op jit(solution)/shard_map/finish/pallas_call | solution.py:223
Async XLA Ops:
  0.6 1.2 %copy-start = (bf16[1,128,4096]{2,1,0:T(8,128)(2,1)S(1)}, bf16[1,128,4096]{2,1,0:T(8,128)(2,1)}, u32[]{:S(2)}) copy-start(bf16[1,128,4096]{2,1,0:T(8,128)(2,1)} %in_ref.1) | copy-start | bytes 3145732
  1.9 1.2 %copy-start.1 = (bf16[1,128,4096]{2,1,0:T(8,128)(2,1)S(1)}, bf16[1,128,4096]{2,1,0:T(8,128)(2,1)}, u32[]{:S(2)}) copy-start(bf16[1,128,4096]{2,1,0:T(8,128)(2,1)} %grad_ref.3) | copy-start | bytes 3145732
  3.1 0.7 %copy-start.4 = (f32[8]{0:T(128)S(1)}, f32[8]{0:T(128)}, u32[]{:S(2)}) copy-start(f32[8]{0:T(128)} %rates_ref.7) | copy-start | bytes 100
  3.7 28.8 %copy-start.2 = (bf16[1,128,4096]{2,1,0:T(8,128)(2,1)S(1)}, bf16[1,128,4096]{2,1,0:T(8,128)(2,1)}, u32[]{:S(2)}) copy-start(bf16[1,128,4096]{2,1,0:T(8,128)(2,1)} %grad_ref.3) | copy-start | bytes 3145732
  3.7 28.8 %copy-start.3 = (f32[8,4096]{1,0:T(8,128)S(1)}, f32[8,4096]{1,0:T(8,128)}, u32[]{:S(2)}) copy-start(f32[8,4096]{1,0:T(8,128)} %residues_ref.3) | copy-start | bytes 393220
  3.7 28.8 %copy-start.5 = (f32[8]{0:T(128)S(1)}, f32[8]{0:T(128)}, u32[]{:S(2)}) copy-start(f32[8]{0:T(128)} %rates_ref.7) | copy-start | bytes 100
  29.9 13.2 %all-to-all-start.1 = ((f32[32,16,128]{2,1,0:T(8,128)}), f32[32,16,128]{2,1,0:T(8,128)S(1)}, u32[]{:S(2)}, u32[]{:S(2)}) async-start(f32[32,16,128]{2,1,0:T(8,128)} %scan.1), calls=%async_computation.1 | async-start | bytes 524288 | tf_op jit(solution)/shard_map/all_to_all | solution.py:222

commit v2 on v1

--- a/solution.py
+++ b/solution.py
@@ -8,6 +8,7 @@
 from jax.sharding import PartitionSpec as P
 
 VMEM_LIMIT = 48 * 1024 * 1024
+FIRST_LIMIT = 60 * 1024 * 1024
 LANES = 128
 
 
@@ -33,40 +34,57 @@
     return jnp.where(lag >= 0.0, table, 0.0).astype(jnp.bfloat16)
 
 
-def terms_kernel(sub, rates_ref, grad_ref, in_ref, out_ref, decay_ref, pair_ref):
-    mode_count = rates_ref.shape[0]
-    rows, width = grad_ref.shape[1:]
-
-    @pl.when(pl.program_id(0) == 0)
-    def _():
-        for r in range(mode_count):
-            decay_ref[r * rows : (r + 1) * rows, :] = decay_matrix(rates_ref[r], rows, False)
-        rates = rate_column(rates_ref, mode_count, rows)
-        offset = lax.broadcasted_iota(jnp.int32, (mode_count, rows), 1).astype(jnp.float32)
-        state = jnp.exp(-rates * offset)
-        carry = mode_gain(rates) * jnp.exp(-rates * (rows - offset))
-        pair_ref[...] = jnp.concatenate([state, carry], axis=0).astype(jnp.bfloat16)
-
-    for first in range(0, width, sub):
-        part = slice(first, first + sub)
-        grad = grad_ref[0, :, part]
-        block = in_ref[0, :, part]
-        state = jnp.dot(pair_ref[...], grad, preferred_element_type=jnp.float32)[:mode_count]
-        carry = jnp.dot(pair_ref[...], block, preferred_element_type=jnp.float32)[mode_count:]
-        grad32 = grad.astype(jnp.float32)
-        sums = []
-        for r in range(mode_count):
-            weighted = jnp.dot(
-                decay_ref[r * rows : (r + 1) * rows, :], block, preferred_element_type=jnp.float32
+def terms_kernel(
+    slices, sub, rates_hbm, grad_hbm, in_hbm, out_ref, rates_ref, grad_ref, in_ref, decay_ref, pair_ref, sems
+):
+    mode_count = rates_ref.shape[0]
+    rows, channels = grad_ref.shape
+    width = channels // slices
+    get_rates = pltpu.make_async_copy(rates_hbm, rates_ref, sems.at[2, 0])
+    get_rates.start()
+    loads = []
+    for i in range(slices):
+        part = pl.ds(i * width, width)
+        pair = (
+            pltpu.make_async_copy(grad_hbm.at[0, :, part], grad_ref.at[:, part], sems.at[0, i]),
+            pltpu.make_async_copy(in_hbm.at[0, :, part], in_ref.at[:, part], sems.at[1, i]),
+        )
+        for copy in pair:
+            copy.start()
+        loads.append(pair)
+    get_rates.wait()
+    for r in range(mode_count):
+        decay_ref[r * rows : (r + 1) * rows, :] = decay_matrix(rates_ref[r], rows, False)
+    rates = rate_column(rates_ref, mode_count, rows)
+    offset = lax.broadcasted_iota(jnp.int32, (mode_count, rows), 1).astype(jnp.float32)
+    state = jnp.exp(-rates * offset)
+    carry = mode_gain(rates) * jnp.exp(-rates * (rows - offset))
+    pair_ref[...] = jnp.concatenate([state, carry], axis=0).astype(jnp.bfloat16)
+
+    for i in range(slices):
+        for copy in loads[i]:
+            copy.wait()
+        for first in range(i * width, (i + 1) * width, sub):
+            part = slice(first, first + sub)
+            grad = grad_ref[:, part]
+            block = in_ref[:, part]
+            state = jnp.dot(pair_ref[...], grad, preferred_element_type=jnp.float32)[:mode_count]
+            carry = jnp.dot(pair_ref[...], block, preferred_element_type=jnp.float32)[mode_count:]
+            grad32 = grad.astype(jnp.float32)
+            weighted = jnp.dot(decay_ref[...], block, preferred_element_type=jnp.float32)
+            local = jnp.concatenate(
+                [
+                    jnp.sum(weighted[r * rows : (r + 1) * rows] * grad32, axis=0, keepdims=True)
+                    for r in range(mode_count)
+                ],
+                axis=0,
             )
-            sums.append(jnp.sum(weighted * grad32, axis=0, keepdims=True))
-        local = jnp.concatenate(sums, axis=0)
-        for k in range(sub // LANES):
-            lanes = slice(k * LANES, (k + 1) * LANES)
-            chunk = first // LANES + k
-            out_ref[chunk, 0:mode_count, :] = state[:, lanes]
-            out_ref[chunk, mode_count : 2 * mode_count, :] = carry[:, lanes]
-            out_ref[chunk, 2 * mode_count : 3 * mode_count, :] = local[:, lanes]
+            for k in range(sub // LANES):
+                lanes = slice(k * LANES, (k + 1) * LANES)
+                chunk = first // LANES + k
+                out_ref[chunk, 0:mode_count, :] = state[:, lanes]
+                out_ref[chunk, mode_count : 2 * mode_count, :] = carry[:, lanes]
+                out_ref[chunk, 2 * mode_count : 3 * mode_count, :] = local[:, lanes]
 
 
 def local_grad_kernel(sub, rates_ref, residues_ref, grad_ref, out_ref, decay_ref):
@@ -118,38 +136,42 @@
     lax.fori_loop(0, batch_count * block_count, spread, 0, unroll=8)
 
 
-def finish_kernel(rates_ref, residues_ref, local_ref, back_ref, grad_ref, sum_ref):
-    mode_count = rates_ref.shape[0]
-    rows, width = local_ref.shape
-    step = pl.program_id(0)
-    chunks = width // LANES
+def finish_kernel(
+    slices, rates_ref, residues_ref, local_ref, back_ref, grad_hbm, sum_ref, grad_ref, sems
+):
+    mode_count = rates_ref.shape[0]
+    rows, channels = local_ref.shape
+    width = channels // slices
     rates = rate_column(rates_ref, mode_count, rows)
     offset = lax.broadcasted_iota(jnp.int32, (mode_count, rows), 1).astype(jnp.float32)
     carry = mode_gain(rates) * jnp.exp(-rates * (rows - offset))
-    carry3 = jnp.concatenate([carry, carry, carry], axis=0).astype(jnp.bfloat16)
-    pieces = []
-    for k in range(chunks):
-        lanes = slice(k * LANES, (k + 1) * LANES)
-        rest = residues_ref[:, lanes] * back_ref[step * chunks + k, 0:mode_count, :]
-        split = []
-        for _ in range(3):
-            split.append(rest.astype(jnp.bfloat16).astype(jnp.float32))
-            rest = rest - split[-1]
-        pieces.append(jnp.concatenate(split, axis=0).astype(jnp.bfloat16))
-    carried = lax.dot_general(
-        carry3,
-        jnp.concatenate(pieces, axis=1),
-        (((0,), (0,)), ((), ())),
-        preferred_element_type=jnp.float32,
-    )
-    grad_ref[0] = (local_ref[...] + carried).astype(jnp.bfloat16)
-
-    @pl.when(step == 0)
-    def _():
-        own = sum_ref.shape[1] // LANES
-        base = lax.axis_index("dp") * own
-        for k in range(own):
-            sum_ref[:, k * LANES : (k + 1) * LANES] = back_ref[base + k, mode_count : 2 * mode_count, :]
+    carry_twice = jnp.concatenate([carry, carry], axis=0).astype(jnp.bfloat16)
+    stores = []
+    for i in range(slices):
+        pieces = []
+        for chunk in range(i * width // LANES, (i + 1) * width // LANES):
+            lanes = slice(chunk * LANES, (chunk + 1) * LANES)
+            value = residues_ref[:, lanes] * back_ref[chunk, 0:mode_count, :]
+            high = value.astype(jnp.bfloat16).astype(jnp.float32)
+            pieces.append(jnp.concatenate([high, value - high], axis=0).astype(jnp.bfloat16))
+        carried = lax.dot_general(
+            carry_twice,
+            jnp.concatenate(pieces, axis=1),
+            (((0,), (0,)), ((), ())),
+            preferred_element_type=jnp.float32,
+        )
+        part = pl.ds(i * width, width)
+        grad_ref[:, part] = (local_ref[:, part] + carried).astype(jnp.bfloat16)
+        stores.append(
+            pltpu.make_async_copy(grad_ref.at[:, part], grad_hbm.at[0, :, part], sems.at[i])
+        )
+        stores[-1].start()
+    own = sum_ref.shape[1] // LANES
+    base = lax.axis_index("dp") * own
+    for k in range(own):
+        sum_ref[:, k * LANES : (k + 1) * LANES] = back_ref[base + k, mode_count : 2 * mode_count, :]
+    for copy in stores:
+        copy.wait()
 
 
 def to_owners(chunks, owners):
@@ -169,8 +191,8 @@
     return jnp.swapaxes(chunks, 1, 2).reshape(count, rows, LANES)
 
 
-def params():
-    return pltpu.CompilerParams(vmem_limit_bytes=VMEM_LIMIT)
+def params(limit=VMEM_LIMIT):
+    return pltpu.CompilerParams(vmem_limit_bytes=limit)
 
 
 def local(batch_count, block_count, grad_out, block_in, residues, decay_rates):
@@ -181,17 +203,22 @@
     width = 1024
     steps = channels // width
     rows_block = pl.BlockSpec((1, rows, width), lambda i: (0, 0, i))
+    anywhere = pl.BlockSpec(memory_space=pl.ANY)
+    whole = pl.BlockSpec(memory_space=pltpu.VMEM)
     terms = pl.pallas_call(
-        functools.partial(terms_kernel, 256),
-        grid=(steps,),
-        in_specs=[smem, rows_block, rows_block],
-        out_specs=pl.BlockSpec((width // LANES, 3 * modes, LANES), lambda i: (i, 0, 0)),
+        functools.partial(terms_kernel, steps, 256),
+        in_specs=[anywhere, anywhere, anywhere],
+        out_specs=whole,
         out_shape=jax.ShapeDtypeStruct((channels // LANES, 3 * modes, LANES), jnp.float32),
         scratch_shapes=[
+            pltpu.SMEM((modes,), jnp.float32),
+            pltpu.VMEM((rows, channels), jnp.bfloat16),
+            pltpu.VMEM((rows, channels), jnp.bfloat16),
             pltpu.VMEM((modes * rows, rows), jnp.bfloat16),
             pltpu.VMEM((2 * modes, rows), jnp.bfloat16),
+            pltpu.SemaphoreType.DMA((3, steps)),
         ],
-        compiler_params=params(),
+        compiler_params=params(FIRST_LIMIT),
         name="terms",
     )(decay_rates, grad_out, block_in)
     terms = lax.all_to_all(to_owners(terms, owners), ("dp", "seq"), 0, 0)
@@ -210,7 +237,6 @@
         ),
         name="local_grad",
     )(decay_rates, residues, grad_out)
-    whole = pl.BlockSpec(memory_space=pltpu.VMEM)
     back = pl.pallas_call(
         functools.partial(scan_kernel, batch_count, block_count),
         in_specs=[smem, whole],
@@ -221,19 +247,14 @@
     )(decay_rates, terms)
     back = from_owners(lax.all_to_all(back, ("dp", "seq"), 0, 0), channels // LANES)
     return pl.pallas_call(
-        finish_kernel,
-        grid=(steps,),
-        in_specs=[
-            smem,
-            pl.BlockSpec((modes, width), lambda i: (0, i)),
-            pl.BlockSpec((rows, width), lambda i: (0, i)),
-            pl.BlockSpec((channels // LANES, 2 * modes, LANES), lambda i: (0, 0, 0)),
-        ],
-        out_specs=[rows_block, pl.BlockSpec((modes, channels // batch_count), lambda i: (0, 0))],
+        functools.partial(finish_kernel, steps),
+        in_specs=[smem, whole, whole, whole],
+        out_specs=[anywhere, whole],
         out_shape=[
             jax.ShapeDtypeStruct((1, rows, channels), jnp.bfloat16),
             jax.ShapeDtypeStruct((modes, channels // batch_count), jnp.float32),
         ],
+        scratch_shapes=[pltpu.VMEM((rows, channels), jnp.bfloat16), pltpu.SemaphoreType.DMA((steps,))],
         compiler_params=params(),
         name="finish",
     )(decay_rates, residues, local_grad, back)

time: 46.4 us -> 44 us (0.948)
  local copies, waits for them, and re-layouts: 3.11 us -> 0.01 us
  Pallas kernels: 11.2 us -> 11.7 us
    unnamed x12 -> x6, local copies, waits for them, and re-layouts: 3.11 us -> 0.01 us
where the time goes in v2:
time: 44 us; the launch traced here: 43.6 us
  blocking collectives  20.9 us (48%)
  Pallas kernels  11.7 us (27%)
  waiting for transfers between devices  7.8 us (18%)
  starting transfers between devices  2.59 us (6%)
  between operations  0.7 us (2%)
    all_to_all x1, blocking collectives, local(): terms = lax.all_to_all(to_owners(terms, owners), ('dp', 'seq'), 0, 0)  20.9 us
    all_to_all x1, waiting for transfers between devices, local(): lax.all_to_all(back, ('dp', 'seq'), 0, 0)  7.8 us
    pallas_call x1, Pallas kernels, local(): pl.pallas_call(functools.partial(terms_kernel, steps, 256), in_specs=[any...  5.12 us
    pallas_call x1, Pallas kernels, local(): pl.pallas_call(functools.partial(local_grad_kernel, 256), grid=(steps,),...  2.82 us
    all_to_all x1, starting transfers between devices, local(): lax.all_to_all(back, ('dp', 'seq'), 0, 0)  2.59 us
    pallas_call x1, Pallas kernels, local(): pl.pallas_call(functools.partial(finish_kernel, steps), in_specs=[smem, w...  2.42 us
    pallas_call x1, Pallas kernels, local(): pl.pallas_call(functools.partial(scan_kernel, batch_count, block_count),...  1.31 us
  transfers between devices with their start and end apart: 1, of which 1 were waited for; matrix products, arithmetic and copies ran while one was open for 0% of the time, Pallas kernels for 6%

profile of v2, /device:TPU:0, one launch (start us, length us, event | category | flops | bytes accessed | tf_op | source)
XLA Modules:
  0.0 43.6 jit_solution(9656868563376769909)
XLA Ops:
  0.6 0.0 copy-start.2
  0.6 0.0 copy-start
  0.7 0.0 copy-start.1
  0.7 5.1 %terms.1 = f32[32,24,128]{2,1,0:T(8,128)} custom-call(f32[8]{0:T(128)} %rates_ref.5, bf16[1,128,4096]{2,1,0:T(8,128)(2,1)} %grad_hbm.1, bf16[1,128,4096]{2,1,0:T(8,128)(2,1)} %in_hbm.1), custom_call_target="tpu_custom_call" | custom-call | tf_op jit(solution)/shard_map/terms/pallas_call | solution.py:208
  5.8 20.9 %all_to_all.10.terms_ref = f32[32,24,128]{2,1,0:T(8,128)S(1)} all-to-all(f32[32,24,128]{2,1,0:T(8,128)} %terms.1), channel_id=1, replica_groups=mesh['dp'=4,'seq'=8] {'dp','seq'}, dimensions={0} | all-to-all | bytes 786432 | tf_op jit(solution)/shard_map/all_to_all | solution.py:224
  26.6 0.0 copy-done.2
  26.7 1.3 %scan.1 = f32[32,16,128]{2,1,0:T(8,128)} custom-call(f32[8]{0:T(128)S(1)} %copy-done.2, f32[32,24,128]{2,1,0:T(8,128)S(1)} %all_to_all.10.terms_ref), custom_call_target="tpu_custom_call" | custom-call | tf_op jit(solution)/shard_map/scan/pallas_call | solution.py:240
  28.0 2.6 %all-to-all-start.1 = ((f32[32,16,128]{2,1,0:T(8,128)}), f32[32,16,128]{2,1,0:T(8,128)S(1)}, u32[]{:S(2)}, u32[]{:S(2)}) async-start(f32[32,16,128]{2,1,0:T(8,128)} %scan.1), calls=%async_computation.1 | async-start | bytes 524288 | tf_op jit(solution)/shard_map/all_to_all | solution.py:248
  30.6 0.0 copy-done
  30.6 0.0 copy-done.1
  30.6 2.8 %local_grad.1.local_ref = f32[128,4096]{1,0:T(8,128)S(1)} custom-call(f32[8]{0:T(128)S(1)} %copy-done.2, f32[8,4096]{1,0:T(8,128)S(1)} %copy-done.1, bf16[1,128,4096]{2,1,0:T(8,128)(2,1)S(1)} %copy-done), custom_call_target="tpu_custom_call" | custom-call | flops 1073741824 | bytes 3145728 | tf_op jit(solution)/shard_map/local_grad/pallas_call | solution.py:225
  33.4 7.8 %all-to-all-done.1.back_ref = f32[32,16,128]{2,1,0:T(8,128)S(1)} async-done(((f32[32,16,128]{2,1,0:T(8,128)}), f32[32,16,128]{2,1,0:T(8,128)S(1)}, u32[]{:S(2)}, u32[]{:S(2)}) %all-to-all-start.1) | async-done | bytes 262176 | tf_op jit(solution)/shard_map/all_to_all | solution.py:248
  41.2 2.4 %finish.1 = (bf16[1,128,4096]{2,1,0:T(8,128)(2,1)}, f32[8,1024]{1,0:T(8,128)}) custom-call(f32[8]{0:T(128)S(1)} %copy-done.2, f32[8,4096]{1,0:T(8,128)S(1)} %copy-done.1, f32[128,4096]{1,0:T(8,128)S(1)} %local_grad.1.local_ref, f32[32,16,128]{2,1,0:T(8,128)S(1)} %all-to-all-done.1.back_ref), custom_call_target="tpu_custom_call" | custom-call | tf_op jit(solution)/shard_map/finish/pallas_call | solution.py:249
Async XLA Ops:
  0.6 26.0 %copy-start.2 = (f32[8]{0:T(128)S(1)}, f32[8]{0:T(128)}, u32[]{:S(2)}) copy-start(f32[8]{0:T(128)} %rates_ref.5) | copy-start | bytes 100
  0.6 29.9 %copy-start = (bf16[1,128,4096]{2,1,0:T(8,128)(2,1)S(1)}, bf16[1,128,4096]{2,1,0:T(8,128)(2,1)}, u32[]{:S(2)}) copy-start(bf16[1,128,4096]{2,1,0:T(8,128)(2,1)} %grad_hbm.1) | copy-start | bytes 3145732
  0.7 29.9 %copy-start.1 = (f32[8,4096]{1,0:T(8,128)S(1)}, f32[8,4096]{1,0:T(8,128)}, u32[]{:S(2)}) copy-start(f32[8,4096]{1,0:T(8,128)} %residues_ref.3) | copy-start | bytes 393220
  28.0 13.2 %all-to-all-start.1 = ((f32[32,16,128]{2,1,0:T(8,128)}), f32[32,16,128]{2,1,0:T(8,128)S(1)}, u32[]{:S(2)}, u32[]{:S(2)}) async-start(f32[32,16,128]{2,1,0:T(8,128)} %scan.1), calls=%async_computation.1 | async-start | bytes 524288 | tf_op jit(solution)/shard_map/all_to_all | solution.py:248

commit v3 on v2

v3 whole, which is shorter than its diff:
```python
import functools

import jax
import jax.numpy as jnp
from jax import lax
from jax.experimental import pallas as pl
from jax.experimental.pallas import tpu as pltpu
from jax.sharding import PartitionSpec as P

VMEM_LIMIT = 48 * 1024 * 1024
FIRST_LIMIT = 60 * 1024 * 1024
LANES = 128
SUBLANES = 8
GROUP = 4


def rate_column(rates_ref, mode_count, width):
    rows = lax.broadcasted_iota(jnp.int32, (mode_count, width), 0)
    column = jnp.zeros((mode_count, width), jnp.float32)
    for r in range(mode_count):
        column = jnp.where(rows == r, rates_ref[r], column)
    return column


def mode_gain(rates):
    return jnp.sqrt(1.0 - jnp.exp(-2.0 * rates))


def decay_matrix(rate, rows):
    earlier = lax.broadcasted_iota(jnp.int32, (rows, rows), 0)
    later = lax.broadcasted_iota(jnp.int32, (rows, rows), 1)
    lag = (later - earlier).astype(jnp.float32)
    rates = jnp.full((rows, rows), rate, jnp.float32)
    gain = mode_gain(jnp.full((SUBLANES, rows), rate, jnp.float32))[:1]
    table = gain * jnp.exp(-rates * jnp.maximum(lag, 0.0))
    return jnp.where(lag >= 0.0, table, 0.0).astype(jnp.bfloat16)


def split_bf16(value):
    high = value.astype(jnp.bfloat16)
    return high, (value - high.astype(jnp.float32)).astype(jnp.bfloat16)


def terms_kernel(
    slices,
    sub,
    rates_hbm,
    grad_hbm,
    in_hbm,
    out_ref,
    rates_ref,
    grad_ref,
    in_ref,
    before_ref,
    after_ref,
    lag_ref,
    sems,
):
    modes = rates_ref.shape[0]
    rows, channels = grad_ref.shape
    width = channels // slices
    groups = rows // GROUP
    get_rates = pltpu.make_async_copy(rates_hbm, rates_ref, sems.at[2, 0])
    get_rates.start()
    loads = []
    for i in range(slices):
        part = pl.ds(i * width, width)
        pair = (
            pltpu.make_async_copy(grad_hbm.at[0, :, part], grad_ref.at[:, part], sems.at[0, i]),
            pltpu.make_async_copy(in_hbm.at[0, :, part], in_ref.at[:, part], sems.at[1, i]),
        )
        for copy in pair:
            copy.start()
        loads.append(pair)
    get_rates.wait()
    rates = rate_column(rates_ref, modes, rows)
    gain = mode_gain(rates)
    position = lax.broadcasted_iota(jnp.int32, (modes, rows), 1)
    offset = position.astype(jnp.float32)
    for u in range(1, groups + 1):
        at = slice((u - 1) * modes, u * modes)
        edge = u * GROUP
        before = gain * jnp.exp(-rates * jnp.maximum(edge - offset, 0.0))
        if u < groups:
            after = jnp.exp(-rates * jnp.maximum(offset - edge, 0.0))
            after = jnp.where((position >= edge) & (position < edge + GROUP), after, 0.0)
            high, low = split_bf16(jnp.where(position < edge, before, 0.0))
            after_high, after_low = split_bf16(after)
        else:
            high, low = before.astype(jnp.bfloat16), jnp.zeros((modes, rows), jnp.bfloat16)
            after_high, after_low = jnp.exp(-rates * offset).astype(jnp.bfloat16), low
        before_ref[at, 0:rows] = high
        before_ref[at, rows : 2 * rows] = low
        after_ref[at, 0:rows] = after_high
        after_ref[at, rows : 2 * rows] = after_low
    for k in range(GROUP):
        lag_ref[k] = (gain * jnp.exp(-rates * k))[:, :LANES]

    in_group = lax.broadcasted_iota(jnp.int32, (SUBLANES, sub), 0) % GROUP
    for i in range(slices):
        for copy in loads[i]:
            copy.wait()
        for first in range(i * width, (i + 1) * width, sub):
            part = slice(first, first + sub)
            grad = grad_ref[:, part]
            block = in_ref[:, part]
            twice = jnp.concatenate([block, block], axis=0)
            sums = jnp.dot(before_ref[...], twice, preferred_element_type=jnp.float32)
            twice = jnp.concatenate([grad, grad], axis=0)
            states = jnp.dot(after_ref[...], twice, preferred_element_type=jnp.float32)
            last = slice((groups - 1) * modes, groups * modes)
            carry, state = sums[last], states[last]
            local = sums[0:modes] * states[0:modes]
            for u in range(1, groups - 1):
                at = slice(u * modes, (u + 1) * modes)
                local = local + sums[at] * states[at]
            grad32 = grad.astype(jnp.float32).reshape(rows // SUBLANES, SUBLANES, sub)
            block32 = block.astype(jnp.float32).reshape(rows // SUBLANES, SUBLANES, sub)
            for k in range(GROUP):
                later = pltpu.roll(grad32, SUBLANES - k, 1) if k else grad32
                product = jnp.sum(block32 * later, axis=0)
                if k:
                    product = jnp.where(in_group + k < GROUP, product, 0.0)
                weight = jnp.concatenate([lag_ref[k]] * (sub // LANES), axis=1)
                local = local + weight * jnp.sum(product, axis=0, keepdims=True)
            for k in range(sub // LANES):
                lanes = slice(k * LANES, (k + 1) * LANES)
                chunk = first // LANES + k
                out_ref[chunk, 0:modes, :] = state[:, lanes]
                out_ref[chunk, modes : 2 * modes, :] = carry[:, lanes]
                out_ref[chunk, 2 * modes : 3 * modes, :] = local[:, lanes]


def local_grad_kernel(
    sub, rates_hbm, residues_ref, grad_hbm, out_ref, rates_ref, grad_ref, decay_ref, sems
):
    modes = rates_ref.shape[0]
    rows, channels = grad_ref.shape
    get_rates = pltpu.make_async_copy(rates_hbm, rates_ref, sems.at[0])
    get_rates.start()
    get_grad = pltpu.make_async_copy(grad_hbm.at[0], grad_ref, sems.at[1])
    get_grad.start()
    get_rates.wait()
    for r in range(modes):
        decay_ref[:, r * rows : (r + 1) * rows] = decay_matrix(rates_ref[r], rows)
    column = lax.broadcasted_iota(jnp.int32, (rows, LANES), 1) % modes
    rates = jnp.zeros((rows, LANES), jnp.float32)
    for r in range(modes):
        rates = jnp.where(column == r, rates_ref[r], rates)
    offset = lax.broadcasted_iota(jnp.int32, (rows, LANES), 0).astype(jnp.float32)
    out_ref[:, channels : channels + LANES] = mode_gain(rates) * jnp.exp(-rates * (rows - offset))
    rates = rate_column(rates_ref, modes, LANES)
    out_ref[0:modes, channels + LANES : channels + 2 * LANES] = jnp.exp(-rates * rows)
    get_grad.wait()

    @pl.loop(0, channels // sub)
    def _(i):
        part = pl.ds(pl.multiple_of(i * sub, sub), sub)
        grad32 = grad_ref[:, part].astype(jnp.float32)
        scaled = jnp.concatenate(
            [(grad32 * residues_ref[r : r + 1, part]).astype(jnp.bfloat16) for r in range(modes)],
            axis=0,
        )
        out_ref[:, part] = jnp.dot(decay_ref[...], scaled, preferred_element_type=jnp.float32)


def scan_kernel(batch_count, block_count, local_ref, terms_ref, out_ref):
    mode_count = out_ref.shape[1] // 2
    width = terms_ref.shape[2]
    last = local_ref.shape[1] - LANES
    decay = local_ref[0:mode_count, last : last + width]
    zero = jnp.zeros((mode_count, width), jnp.float32)

    def sequence(b, total):
        def block(j, state):
            total, incoming = state
            at = (b + 1) * block_count - 1 - j
            out_ref[at, 0:mode_count, :] = incoming
            carry = terms_ref[at, mode_count : 2 * mode_count, :]
            total = total + (terms_ref[at, 2 * mode_count : 3 * mode_count, :] + incoming * carry)
            return total, terms_ref[at, 0:mode_count, :] + decay * incoming

        return lax.fori_loop(0, block_count, block, (total, zero), unroll=block_count <= 8)[0]

    total = lax.fori_loop(0, batch_count, sequence, zero, unroll=batch_count <= 8)

    def spread(at, carry):
        out_ref[at, mode_count : 2 * mode_count, :] = total
        return carry

    lax.fori_loop(0, batch_count * block_count, spread, 0, unroll=8)


def finish_kernel(slices, residues_ref, local_ref, back_ref, grad_hbm, sum_ref, grad_ref, sems):
    modes, channels = residues_ref.shape
    rows = local_ref.shape[0]
    width = channels // slices
    carry = local_ref[:, channels : channels + 2 * modes].astype(jnp.bfloat16)
    stores = []
    for i in range(slices):
        pieces = []
        for chunk in range(i * width // LANES, (i + 1) * width // LANES):
            lanes = slice(chunk * LANES, (chunk + 1) * LANES)
            value = residues_ref[:, lanes] * back_ref[chunk, 0:modes, :]
            high = value.astype(jnp.bfloat16).astype(jnp.float32)
            pieces.append(jnp.concatenate([high, value - high], axis=0).astype(jnp.bfloat16))
        carried = jnp.dot(
            carry, jnp.concatenate(pieces, axis=1), preferred_element_type=jnp.float32
        )
        part = pl.ds(i * width, width)
        grad_ref[:, part] = (local_ref[:, part] + carried).astype(jnp.bfloat16)
        stores.append(
            pltpu.make_async_copy(grad_ref.at[:, part], grad_hbm.at[0, :, part], sems.at[i])
        )
        stores[-1].start()
    own = sum_ref.shape[1] // LANES
    base = lax.axis_index("dp") * own
    for k in range(own):
        sum_ref[:, k * LANES : (k + 1) * LANES] = back_ref[base + k, modes : 2 * modes, :]
    for copy in stores:
        copy.wait()


def to_owners(chunks, owners):
    count, rows, lanes = chunks.shape
    if owners == count:
        return chunks
    narrow = count * lanes // owners
    parts = chunks.reshape(count, rows, lanes // narrow, narrow)
    return jnp.swapaxes(parts, 1, 2).reshape(owners, rows, narrow)


def from_owners(parts, count):
    owners, rows, narrow = parts.shape
    if owners == count:
        return parts
    chunks = parts.reshape(count, owners // count, rows, narrow)
    return jnp.swapaxes(chunks, 1, 2).reshape(count, rows, LANES)


def params(limit=VMEM_LIMIT):
    return pltpu.CompilerParams(vmem_limit_bytes=limit)


def local(batch_count, block_count, grad_out, block_in, residues, decay_rates):
    _, rows, channels = grad_out.shape
    modes = residues.shape[0]
    owners = batch_count * block_count
    chunks = channels // LANES
    anywhere = pl.BlockSpec(memory_space=pl.ANY)
    whole = pl.BlockSpec(memory_space=pltpu.VMEM)
    terms = pl.pallas_call(
        functools.partial(terms_kernel, 2, 256),
        in_specs=[anywhere] * 3,
        out_specs=whole,
        out_shape=jax.ShapeDtypeStruct((chunks, 3 * modes, LANES), jnp.float32),
        scratch_shapes=[
            pltpu.SMEM((modes,), jnp.float32),
            pltpu.VMEM((rows, channels), jnp.bfloat16),
            pltpu.VMEM((rows, channels), jnp.bfloat16),
            pltpu.VMEM((modes * rows // GROUP, 2 * rows), jnp.bfloat16),
            pltpu.VMEM((modes * rows // GROUP, 2 * rows), jnp.bfloat16),
            pltpu.VMEM((GROUP, modes, LANES), jnp.float32),
            pltpu.SemaphoreType.DMA((3, 2)),
        ],
        compiler_params=params(FIRST_LIMIT),
        name="terms",
    )(decay_rates, grad_out, block_in)
    terms = lax.all_to_all(to_owners(terms, owners), ("dp", "seq"), 0, 0)
    local_grad = pl.pallas_call(
        functools.partial(local_grad_kernel, 512),
        in_specs=[anywhere, whole, anywhere],
        out_specs=whole,
        out_shape=jax.ShapeDtypeStruct((rows, channels + 2 * LANES), jnp.float32),
        scratch_shapes=[
            pltpu.SMEM((modes,), jnp.float32),
            pltpu.VMEM((rows, channels), jnp.bfloat16),
            pltpu.VMEM((rows, modes * rows), jnp.bfloat16),
            pltpu.SemaphoreType.DMA((2,)),
        ],
        compiler_params=params(),
        cost_estimate=pl.CostEstimate(
            flops=2 * rows * modes * rows * channels,
            bytes_accessed=6 * rows * channels,
            transcendentals=0,
        ),
        name="local_grad",
    )(decay_rates, residues, grad_out)
    back = pl.pallas_call(
        functools.partial(scan_kernel, batch_count, block_count),
        in_specs=[whole, whole],
        out_specs=whole,
        out_shape=jax.ShapeDtypeStruct((owners, 2 * modes, channels // owners), jnp.float32),
        compiler_params=params(),
        name="scan",
    )(local_grad, terms)
    back = from_owners(lax.all_to_all(back, ("dp", "seq"), 0, 0), chunks)
    return pl.pallas_call(
        functools.partial(finish_kernel, 4),
        in_specs=[whole] * 3,
        out_specs=[anywhere, whole],
        out_shape=[
            jax.ShapeDtypeStruct((1, rows, channels), jnp.bfloat16),
            jax.ShapeDtypeStruct((modes, channels // batch_count), jnp.float32),
        ],
        scratch_shapes=[pltpu.VMEM((rows, channels), jnp.bfloat16), pltpu.SemaphoreType.DMA((4,))],
        compiler_params=params(),
        name="finish",
    )(residues, local_grad, back)


def solution(mesh):
    placed = (P("dp", "seq", None), P("dp", "seq", None), P(), P())
    return jax.shard_map(
        functools.partial(local, mesh.shape["dp"], mesh.shape["seq"]),
        mesh=mesh,
        in_specs=placed,
        out_specs=(P("dp", "seq", None), P(None, "dp")),
        check_vma=False,
    )
```

time: 44 us -> 39.9 us (0.907)
  blocking collectives: 20.9 us -> 12.7 us
  starting transfers between devices: 2.59 us -> 7.3 us
  Pallas kernels: 11.7 us -> 8.71 us
  local copies, waits for them, and re-layouts: 0.01 us -> 1.23 us
  waiting for transfers between devices: 7.8 us -> 8.99 us
    all_to_all x1, blocking collectives: 20.9 us -> 12.7 us  [local(): back = from_owners(lax.all_to_all(back, ('dp', 'seq'), 0, 0), chunks)]
    all_to_all x1, starting transfers between devices: 2.59 us -> 7.3 us  [local(): terms = lax.all_to_all(to_owners(terms, owners), ('dp', 'seq'), 0, 0)]
    pallas_call x3, Pallas kernels: 10.4 us -> 8.65 us  [the longest x1 3.54 us: local(): pl.pallas_call(functools.partial(terms_kernel, 2, 256), in_specs=[anywher...]
    pallas_call x1, Pallas kernels: 1.31 us -> 0.05 us  [local(): pl.pallas_call(functools.partial(scan_kernel, batch_count, block_count),...]
    unnamed x6, local copies, waits for them, and re-layouts: 0.01 us -> 1.23 us
    all_to_all x1, waiting for transfers between devices: 7.8 us -> 8.99 us  [local(): terms = lax.all_to_all(to_owners(terms, owners), ('dp', 'seq'), 0, 0)]
  transfers between devices with their start and end apart: 1 -> 1, of which waited for: 1 -> 1; matrix products, arithmetic and copies ran while one was open for 0% -> 0% of each run, Pallas kernels for 6% -> 8%
where the time goes in v3:
time: 39.9 us; the launch traced here: 39.7 us
  blocking collectives  12.7 us (32%)
  waiting for transfers between devices  8.99 us (23%)
  Pallas kernels  8.71 us (22%)
  starting transfers between devices  7.3 us (18%)
  local copies, waits for them, and re-layouts  1.23 us (3%)
  between operations  0.7 us (2%)
    all_to_all x1, blocking collectives, local(): back = from_owners(lax.all_to_all(back, ('dp', 'seq'), 0, 0), chunks)  12.7 us
    all_to_all x1, waiting for transfers between devices, local(): terms = lax.all_to_all(to_owners(terms, owners), ('dp', 'seq'), 0, 0)  8.99 us
    all_to_all x1, starting transfers between devices, local(): terms = lax.all_to_all(to_owners(terms, owners), ('dp', 'seq'), 0, 0)  7.3 us
    pallas_call x1, Pallas kernels, local(): pl.pallas_call(functools.partial(terms_kernel, 2, 256), in_specs=[anywher...  3.54 us
    pallas_call x1, Pallas kernels, local(): pl.pallas_call(functools.partial(local_grad_kernel, 512), in_specs=[anywh...  3.3 us
    pallas_call x1, Pallas kernels, local(): pl.pallas_call(functools.partial(finish_kernel, 4), in_specs=[whole] * 3,...  1.82 us
    unnamed x6, local copies, waits for them, and re-layouts  1.23 us
  transfers between devices with their start and end apart: 1, of which 1 were waited for; matrix products, arithmetic and copies ran while one was open for 0% of the time, Pallas kernels for 8%

profile of v3, /device:TPU:0, one launch (start us, length us, event | category | flops | bytes accessed | tf_op | source)
XLA Modules:
  0.0 39.7 jit_solution(9980756908405499893)
XLA Ops:
  0.6 0.0 copy-start.2
  0.6 0.0 copy-start.1
  0.7 3.5 %terms.1 = f32[32,24,128]{2,1,0:T(8,128)} custom-call(f32[8]{0:T(128)} %rates_hbm.3, bf16[1,128,4096]{2,1,0:T(8,128)(2,1)} %grad_hbm.3, bf16[1,128,4096]{2,1,0:T(8,128)(2,1)} %in_hbm.1), custom_call_target="tpu_custom_call" | custom-call | tf_op jit(solution)/shard_map/terms/pallas_call | solution.py:252
  4.2 7.3 %all-to-all-start = ((f32[32,24,128]{2,1,0:T(8,128)}), f32[32,24,128]{2,1,0:T(8,128)S(1)}, u32[]{:S(2)}, u32[]{:S(2)}) async-start(f32[32,24,128]{2,1,0:T(8,128)} %terms.1), calls=%async_computation | async-start | bytes 786432 | tf_op jit(solution)/shard_map/all_to_all | solution.py:269
  11.5 0.0 copy-done.2
  11.5 0.0 copy-done.1
  11.5 0.0 copy-start
  11.5 1.2 %copy-done = bf16[1,128,4096]{2,1,0:T(8,128)(2,1)S(1)} copy-done((bf16[1,128,4096]{2,1,0:T(8,128)(2,1)S(1)}, bf16[1,128,4096]{2,1,0:T(8,128)(2,1)}, u32[]{:S(2)}) %copy-start) | copy-done | bytes 1048600
  12.8 3.3 %local_grad.1.local_ref = f32[128,4352]{1,0:T(8,128)S(1)} custom-call(f32[8]{0:T(128)S(1)} %copy-done.2, f32[8,4096]{1,0:T(8,128)S(1)} %copy-done.1, bf16[1,128,4096]{2,1,0:T(8,128)(2,1)S(1)} %copy-done), custom_call_target="tpu_custom_call" | custom-call | flops 1073741824 | bytes 3145728 | tf_op jit(solution)/shard_map/local_grad/pallas_call | solution.py:270
  16.1 9.0 %all-to-all-done.terms_ref = f32[32,24,128]{2,1,0:T(8,128)S(1)} async-done(((f32[32,24,128]{2,1,0:T(8,128)}), f32[32,24,128]{2,1,0:T(8,128)S(1)}, u32[]{:S(2)}, u32[]{:S(2)}) %all-to-all-start) | async-done | bytes 393248 | tf_op jit(solution)/shard_map/all_to_all | solution.py:269
  25.0 0.1 scan.1
  25.1 12.7 %all_to_all.10.back_ref = f32[32,16,128]{2,1,0:T(8,128)S(1)} all-to-all(f32[32,16,128]{2,1,0:T(8,128)S(1)} %scan.1), channel_id=1, replica_groups=mesh['dp'=4,'seq'=8] {'dp','seq'}, dimensions={0} | all-to-all | bytes 524288 | tf_op jit(solution)/shard_map/all_to_all | solution.py:297
  37.8 1.8 %finish.1 = (bf16[1,128,4096]{2,1,0:T(8,128)(2,1)}, f32[8,1024]{1,0:T(8,128)}) custom-call(f32[8,4096]{1,0:T(8,128)S(1)} %copy-done.1, f32[128,4352]{1,0:T(8,128)S(1)} %local_grad.1.local_ref, f32[32,16,128]{2,1,0:T(8,128)S(1)} %all_to_all.10.back_ref), custom_call_target="tpu_custom_call" | custom-call | tf_op jit(solution)/shard_map/finish/pallas_call | solution.py:298
Async XLA Ops:
  0.6 10.9 %copy-start.2 = (f32[8]{0:T(128)S(1)}, f32[8]{0:T(128)}, u32[]{:S(2)}) copy-start(f32[8]{0:T(128)} %rates_hbm.3) | copy-start | bytes 100
  0.6 10.9 %copy-start.1 = (f32[8,4096]{1,0:T(8,128)S(1)}, f32[8,4096]{1,0:T(8,128)}, u32[]{:S(2)}) copy-start(f32[8,4096]{1,0:T(8,128)} %residues_ref.3) | copy-start | bytes 393220
  4.2 20.9 %all-to-all-start = ((f32[32,24,128]{2,1,0:T(8,128)}), f32[32,24,128]{2,1,0:T(8,128)S(1)}, u32[]{:S(2)}, u32[]{:S(2)}) async-start(f32[32,24,128]{2,1,0:T(8,128)} %terms.1), calls=%async_computation | async-start | bytes 786432 | tf_op jit(solution)/shard_map/all_to_all | solution.py:269
  11.5 1.2 %copy-start = (bf16[1,128,4096]{2,1,0:T(8,128)(2,1)S(1)}, bf16[1,128,4096]{2,1,0:T(8,128)(2,1)}, u32[]{:S(2)}) copy-start(bf16[1,128,4096]{2,1,0:T(8,128)(2,1)} %grad_hbm.3) | copy-start | bytes 3145732

commit v4 on v3

--- a/solution.py
+++ b/solution.py
@@ -164,31 +164,68 @@
         out_ref[:, part] = jnp.dot(decay_ref[...], scaled, preferred_element_type=jnp.float32)
 
 
-def scan_kernel(batch_count, block_count, local_ref, terms_ref, out_ref):
-    mode_count = out_ref.shape[1] // 2
-    width = terms_ref.shape[2]
+def block_decay(local_ref, modes, width):
     last = local_ref.shape[1] - LANES
-    decay = local_ref[0:mode_count, last : last + width]
-    zero = jnp.zeros((mode_count, width), jnp.float32)
-
-    def sequence(b, total):
-        def block(j, state):
-            total, incoming = state
-            at = (b + 1) * block_count - 1 - j
-            out_ref[at, 0:mode_count, :] = incoming
-            carry = terms_ref[at, mode_count : 2 * mode_count, :]
-            total = total + (terms_ref[at, 2 * mode_count : 3 * mode_count, :] + incoming * carry)
-            return total, terms_ref[at, 0:mode_count, :] + decay * incoming
-
-        return lax.fori_loop(0, block_count, block, (total, zero), unroll=block_count <= 8)[0]
-
-    total = lax.fori_loop(0, batch_count, sequence, zero, unroll=batch_count <= 8)
-
-    def spread(at, carry):
-        out_ref[at, mode_count : 2 * mode_count, :] = total
-        return carry
-
-    lax.fori_loop(0, batch_count * block_count, spread, 0, unroll=8)
+    return local_ref[0:modes, last : last + width]
+
+
+def steps(count, body, start):
+    return lax.fori_loop(0, count, body, start, unroll=count <= 8)
+
+
+def half_kernel(batch_count, half, local_ref, terms_ref, out_ref):
+    modes, width = out_ref.shape[1:]
+    pieces = terms_ref.shape[0] // (batch_count * half)
+    decay = block_decay(local_ref, modes, width)
+    zero = jnp.zeros((modes, width), jnp.float32)
+    later = lax.axis_index("seq") >= half
+    for k in range(pieces):
+
+        def sequence(b, total):
+            def state(j, pair):
+                total, incoming = pair
+                at = (b * half + half - 1 - j) * pieces + k
+                weights = terms_ref[at, modes : 2 * modes, :]
+                total = total + (terms_ref[at, 2 * modes : 3 * modes, :] + incoming * weights)
+                return total, terms_ref[at, 0:modes, :] + decay * incoming
+
+            def weight(j, before):
+                return terms_ref[(b * half + j) * pieces + k, modes : 2 * modes, :] + decay * before
+
+            total, incoming = steps(half, state, (total, zero))
+            out_ref[b * pieces + k] = jnp.where(later, incoming, steps(half, weight, zero))
+            return total
+
+        out_ref[batch_count * pieces + k] = steps(batch_count, sequence, zero)
+
+
+def scan_kernel(batch_count, half, local_ref, terms_ref, own_ref, other_ref, out_ref):
+    modes, width = own_ref.shape[1:]
+    pieces = terms_ref.shape[0] // (batch_count * half)
+    decay = block_decay(local_ref, modes, width)
+    later = lax.axis_index("seq") >= half
+    for k in range(pieces):
+        last = batch_count * pieces + k
+        total = own_ref[last] + other_ref[last]
+
+        def sequence(b, total):
+            other = other_ref[b * pieces + k]
+
+            def block(j, incoming):
+                at = (b * half + half - 1 - j) * pieces + k
+                out_ref[at, 0:modes, :] = incoming
+                return terms_ref[at, 0:modes, :] + decay * incoming
+
+            steps(half, block, jnp.where(later, 0.0, other))
+            return total + own_ref[b * pieces + k] * other
+
+        total = steps(batch_count, sequence, total)
+
+        def spread(i, carry):
+            out_ref[i * pieces + k, modes : 2 * modes, :] = total
+            return carry
+
+        lax.fori_loop(0, batch_count * half, spread, 0, unroll=8)
 
 
 def finish_kernel(slices, residues_ref, local_ref, back_ref, grad_hbm, sum_ref, grad_ref, sems):
@@ -223,8 +260,8 @@
 
 def to_owners(chunks, owners):
     count, rows, lanes = chunks.shape
-    if owners == count:
-        return chunks
+    if owners <= count:
+        return chunks.reshape(owners, count // owners * rows, lanes)
     narrow = count * lanes // owners
     parts = chunks.reshape(count, rows, lanes // narrow, narrow)
     return jnp.swapaxes(parts, 1, 2).reshape(owners, rows, narrow)
@@ -232,8 +269,8 @@
 
 def from_owners(parts, count):
     owners, rows, narrow = parts.shape
-    if owners == count:
-        return parts
+    if owners <= count:
+        return parts.reshape(count, owners * rows // count, narrow)
     chunks = parts.reshape(count, owners // count, rows, narrow)
     return jnp.swapaxes(chunks, 1, 2).reshape(count, rows, LANES)
 
@@ -245,8 +282,19 @@
 def local(batch_count, block_count, grad_out, block_in, residues, decay_rates):
     _, rows, channels = grad_out.shape
     modes = residues.shape[0]
-    owners = batch_count * block_count
+    half = block_count // 2
+    owners = batch_count * half
     chunks = channels // LANES
+    width = min(LANES, channels // owners)
+    pieces = channels // (owners * width)
+    groups = [
+        [d * block_count + first + j for d in range(batch_count) for j in range(half)]
+        for first in (0, half)
+    ]
+
+    def exchange(slots):
+        return lax.all_to_all(slots, ("dp", "seq"), 0, 0, axis_index_groups=groups)
+
     anywhere = pl.BlockSpec(memory_space=pl.ANY)
     whole = pl.BlockSpec(memory_space=pltpu.VMEM)
     terms = pl.pallas_call(
@@ -266,7 +314,7 @@
         compiler_params=params(FIRST_LIMIT),
         name="terms",
     )(decay_rates, grad_out, block_in)
-    terms = lax.all_to_all(to_owners(terms, owners), ("dp", "seq"), 0, 0)
+    terms = exchange(to_owners(terms, owners)).reshape(owners * pieces, 3 * modes, width)
     local_grad = pl.pallas_call(
         functools.partial(local_grad_kernel, 512),
         in_specs=[anywhere, whole, anywhere],
@@ -286,15 +334,24 @@
         ),
         name="local_grad",
     )(decay_rates, residues, grad_out)
-    back = pl.pallas_call(
-        functools.partial(scan_kernel, batch_count, block_count),
+    cross = pl.pallas_call(
+        functools.partial(half_kernel, batch_count, half),
         in_specs=[whole, whole],
         out_specs=whole,
-        out_shape=jax.ShapeDtypeStruct((owners, 2 * modes, channels // owners), jnp.float32),
+        out_shape=jax.ShapeDtypeStruct(((batch_count + 1) * pieces, modes, width), jnp.float32),
+        compiler_params=params(),
+        name="half",
+    )(local_grad, terms)
+    other = lax.ppermute(cross, "seq", [(s, (s + half) % block_count) for s in range(block_count)])
+    back = pl.pallas_call(
+        functools.partial(scan_kernel, batch_count, half),
+        in_specs=[whole] * 4,
+        out_specs=whole,
+        out_shape=jax.ShapeDtypeStruct((owners * pieces, 2 * modes, width), jnp.float32),
         compiler_params=params(),
         name="scan",
-    )(local_grad, terms)
-    back = from_owners(lax.all_to_all(back, ("dp", "seq"), 0, 0), chunks)
+    )(local_grad, terms, cross, other)
+    back = from_owners(exchange(back.reshape(owners, pieces * 2 * modes, width)), chunks)
     return pl.pallas_call(
         functools.partial(finish_kernel, 4),
         in_specs=[whole] * 3,

time: 39.9 us -> 36.2 us (0.907)
  blocking collectives: 12.7 us -> 9.74 us
  waiting for transfers between devices: 8.99 us -> 6.49 us
  starting transfers between devices: 7.3 us -> 8.95 us
    all_to_all x1, waiting for transfers between devices: 8.99 us -> 3.48 us  [exchange(): return lax.all_to_all(slots, ('dp', 'seq'), 0, 0, axis_index_groups=groups)]
    ppermute x0 -> x1, waiting for transfers between devices: none -> 3 us  [local(): lax.ppermute(cross, 'seq', [(s, (s + half) % block_count) for s in range(...]
    all_to_all x1, blocking collectives: 12.7 us -> 9.74 us  [exchange(): return lax.all_to_all(slots, ('dp', 'seq'), 0, 0, axis_index_groups=groups)]
    ppermute x0 -> x1, starting transfers between devices: none -> 2.66 us  [local(): lax.ppermute(cross, 'seq', [(s, (s + half) % block_count) for s in range(...]
    all_to_all x1, starting transfers between devices: 7.3 us -> 6.3 us  [exchange(): return lax.all_to_all(slots, ('dp', 'seq'), 0, 0, axis_index_groups=groups)]
  transfers between devices with their start and end apart: 1 -> 2, of which waited for: 1 -> 2; matrix products, arithmetic and copies ran while one was open for 0% -> 0% of each run, Pallas kernels for 8% -> 9%
where the time goes in v4:
time: 36.2 us; the launch traced here: 35.8 us
  blocking collectives  9.74 us (27%)
  starting transfers between devices  8.95 us (25%)
  Pallas kernels  8.72 us (24%)
  waiting for transfers between devices  6.49 us (18%)
  local copies, waits for them, and re-layouts  1.23 us (3%)
  between operations  0.71 us (2%)
    all_to_all x1, blocking collectives, exchange(): return lax.all_to_all(slots, ('dp', 'seq'), 0, 0, axis_index_groups=groups)  9.74 us
    all_to_all x1, starting transfers between devices, exchange(): return lax.all_to_all(slots, ('dp', 'seq'), 0, 0, axis_index_groups=groups)  6.3 us
    pallas_call x1, Pallas kernels, local(): pl.pallas_call(functools.partial(terms_kernel, 2, 256), in_specs=[anywher...  3.54 us
    all_to_all x1, waiting for transfers between devices, exchange(): return lax.all_to_all(slots, ('dp', 'seq'), 0, 0, axis_index_groups=groups)  3.48 us
    pallas_call x1, Pallas kernels, local(): pl.pallas_call(functools.partial(local_grad_kernel, 512), in_specs=[anywh...  3.29 us
    ppermute x1, waiting for transfers between devices, local(): lax.ppermute(cross, 'seq', [(s, (s + half) % block_count) for s in range(...  3 us
    ppermute x1, starting transfers between devices, local(): lax.ppermute(cross, 'seq', [(s, (s + half) % block_count) for s in range(...  2.66 us
    pallas_call x1, Pallas kernels, local(): pl.pallas_call(functools.partial(finish_kernel, 4), in_specs=[whole] * 3,...  1.81 us
  transfers between devices with their start and end apart: 2, of which 2 were waited for; matrix products, arithmetic and copies ran while one was open for 0% of the time, Pallas kernels for 9%

profile of v4, /device:TPU:0, one launch (start us, length us, event | category | flops | bytes accessed | tf_op | source)
XLA Modules:
  0.0 35.8 jit_solution(1645453316601560294)
XLA Ops:
  0.6 0.0 copy-start.2
  0.6 0.0 copy-start.1
  0.7 3.5 %terms.1 = f32[32,24,128]{2,1,0:T(8,128)} custom-call(f32[8]{0:T(128)} %rates_hbm.3, bf16[1,128,4096]{2,1,0:T(8,128)(2,1)} %grad_hbm.3, bf16[1,128,4096]{2,1,0:T(8,128)(2,1)} %in_hbm.1), custom_call_target="tpu_custom_call" | custom-call | tf_op jit(solution)/shard_map/terms/pallas_call | solution.py:300
  4.2 6.3 %all-to-all-start = ((f32[16,48,128]{2,1,0:T(8,128)}), f32[16,48,128]{2,1,0:T(8,128)S(1)}, u32[]{:S(2)}, u32[]{:S(2)}) async-start(f32[16,48,128]{2,1,0:T(8,128)} %bitcast.8), calls=%async_computation | async-start | bytes 786432 | tf_op jit(solution)/shard_map/all_to_all | solution.py:296
  10.5 0.0 copy-done.2
  10.5 0.0 copy-done.1
  10.5 0.0 copy-start
  10.5 1.2 %copy-done = bf16[1,128,4096]{2,1,0:T(8,128)(2,1)S(1)} copy-done((bf16[1,128,4096]{2,1,0:T(8,128)(2,1)S(1)}, bf16[1,128,4096]{2,1,0:T(8,128)(2,1)}, u32[]{:S(2)}) %copy-start) | copy-done | bytes 1048600
  11.7 3.3 %local_grad.1.local_ref = f32[128,4352]{1,0:T(8,128)S(1)} custom-call(f32[8]{0:T(128)S(1)} %copy-done.2, f32[8,4096]{1,0:T(8,128)S(1)} %copy-done.1, bf16[1,128,4096]{2,1,0:T(8,128)(2,1)S(1)} %copy-done), custom_call_target="tpu_custom_call" | custom-call | flops 1073741824 | bytes 3145728 | tf_op jit(solution)/shard_map/local_grad/pallas_call | solution.py:318
  15.0 3.5 %all-to-all-done = f32[16,48,128]{2,1,0:T(8,128)S(1)} async-done(((f32[16,48,128]{2,1,0:T(8,128)}), f32[16,48,128]{2,1,0:T(8,128)S(1)}, u32[]{:S(2)}, u32[]{:S(2)}) %all-to-all-start) | async-done | bytes 393248 | tf_op jit(solution)/shard_map/all_to_all | solution.py:296
  18.6 2.7 %collective-permute-start = (f32[10,8,128]{2,1,0:T(8,128)S(1)}, f32[10,8,128]{2,1,0:T(8,128)S(1)}, u32[]{:S(2)}, u32[]{:S(2)}) collective-permute-start(f32[10,8,128]{2,1,0:T(8,128)S(1)} %half.1.own_ref), channel_id=1, source_target_pairs={{0,4},{1,5},{2,6},{3,7},{4,0},{5,1},{6,2},{7,3},{8,12},{9,13},{10,... | collective-permute-start | bytes 122888 | tf_op jit(solution)/shard_map/ppermute | solution.py:345
  21.2 3.0 %collective-permute-done.other_ref = f32[10,8,128]{2,1,0:T(8,128)S(1)} collective-permute-done((f32[10,8,128]{2,1,0:T(8,128)S(1)}, f32[10,8,128]{2,1,0:T(8,128)S(1)}, u32[]{:S(2)}, u32[]{:S(2)}) %collective-permute-start) | collective-permute-done | bytes 40992 | tf_op jit(solution)/shard_map/ppermute | solution.py:345
  24.3 9.7 %all_to_all.10 = f32[16,32,128]{2,1,0:T(8,128)S(1)} all-to-all(f32[16,32,128]{2,1,0:T(8,128)S(1)} %bitcast.7), channel_id=1, replica_groups={{0,1,2,3,8,9,10,11,16,17,18,19,24,25,26,27},{4,5,6,7,12,13,14,15,20,21,..., dimensions={0} | all-to-all | bytes 524288 | tf_op jit(solution)/shard_map/all_to_all | solution.py:296
  34.0 1.8 %finish.1 = (bf16[1,128,4096]{2,1,0:T(8,128)(2,1)}, f32[8,1024]{1,0:T(8,128)}) custom-call(f32[8,4096]{1,0:T(8,128)S(1)} %copy-done.1, f32[128,4352]{1,0:T(8,128)S(1)} %local_grad.1.local_ref, f32[32,16,128]{2,1,0:T(8,128)S(1)} %bitcast.6), custom_call_target="tpu_custom_call" | custom-call | tf_op jit(solution)/shard_map/finish/pallas_call | solution.py:355
  (2 shorter events, 0.1 us)
Async XLA Ops:
  0.6 9.9 %copy-start.2 = (f32[8]{0:T(128)S(1)}, f32[8]{0:T(128)}, u32[]{:S(2)}) copy-start(f32[8]{0:T(128)} %rates_hbm.3) | copy-start | bytes 100
  0.6 9.9 %copy-start.1 = (f32[8,4096]{1,0:T(8,128)S(1)}, f32[8,4096]{1,0:T(8,128)}, u32[]{:S(2)}) copy-start(f32[8,4096]{1,0:T(8,128)} %residues_ref.3) | copy-start | bytes 393220
  4.2 14.3 %all-to-all-start = ((f32[16,48,128]{2,1,0:T(8,128)}), f32[16,48,128]{2,1,0:T(8,128)S(1)}, u32[]{:S(2)}, u32[]{:S(2)}) async-start(f32[16,48,128]{2,1,0:T(8,128)} %bitcast.8), calls=%async_computation | async-start | bytes 786432 | tf_op jit(solution)/shard_map/all_to_all | solution.py:296
  10.5 1.2 %copy-start = (bf16[1,128,4096]{2,1,0:T(8,128)(2,1)S(1)}, bf16[1,128,4096]{2,1,0:T(8,128)(2,1)}, u32[]{:S(2)}) copy-start(bf16[1,128,4096]{2,1,0:T(8,128)(2,1)} %grad_hbm.3) | copy-start | bytes 3145732
  18.6 5.7 %collective-permute-start = (f32[10,8,128]{2,1,0:T(8,128)S(1)}, f32[10,8,128]{2,1,0:T(8,128)S(1)}, u32[]{:S(2)}, u32[]{:S(2)}) collective-permute-start(f32[10,8,128]{2,1,0:T(8,128)S(1)} %half.1.own_ref), channel_id=1, source_target_pairs={{0,4},{1,5},{2,6},{3,7},{4,0},{5,1},{6,2},{7,3},{8,12},{9,13},{10,... | collective-permute-start | bytes 122888 | tf_op jit(solution)/shard_map/ppermute | solution.py:345

commit v5 on v4

--- a/solution.py
+++ b/solution.py
@@ -55,6 +55,8 @@
     after_ref,
     lag_ref,
     sems,
+    stage_ref,
+    out_sems,
 ):
     modes = rates_ref.shape[0]
     rows, channels = grad_ref.shape
@@ -97,6 +99,7 @@
         lag_ref[k] = (gain * jnp.exp(-rates * k))[:, :LANES]
 
     in_group = lax.broadcasted_iota(jnp.int32, (SUBLANES, sub), 0) % GROUP
+    stores = []
     for i in range(slices):
         for copy in loads[i]:
             copy.wait()
@@ -126,9 +129,14 @@
             for k in range(sub // LANES):
                 lanes = slice(k * LANES, (k + 1) * LANES)
                 chunk = first // LANES + k
-                out_ref[chunk, 0:modes, :] = state[:, lanes]
-                out_ref[chunk, modes : 2 * modes, :] = carry[:, lanes]
-                out_ref[chunk, 2 * modes : 3 * modes, :] = local[:, lanes]
+                stage_ref[chunk, 0:modes, :] = state[:, lanes]
+                stage_ref[chunk, modes : 2 * modes, :] = carry[:, lanes]
+                stage_ref[chunk, 2 * modes : 3 * modes, :] = local[:, lanes]
+        span = pl.ds(i * width // LANES, width // LANES)
+        stores.append(pltpu.make_async_copy(stage_ref.at[span], out_ref.at[span], out_sems.at[i]))
+        stores[-1].start()
+    for copy in stores:
+        copy.wait()
 
 
 def local_grad_kernel(
@@ -228,12 +236,17 @@
         lax.fori_loop(0, batch_count * half, spread, 0, unroll=8)
 
 
-def finish_kernel(slices, residues_ref, local_ref, back_ref, grad_hbm, sum_ref, grad_ref, sems):
+def finish_kernel(slices, residues_ref, local_ref, back_ref, grad_hbm, sum_hbm, grad_ref, sum_ref, sems):
     modes, channels = residues_ref.shape
     rows = local_ref.shape[0]
     width = channels // slices
     carry = local_ref[:, channels : channels + 2 * modes].astype(jnp.bfloat16)
-    stores = []
+    own = sum_ref.shape[1] // LANES
+    base = lax.axis_index("dp") * own
+    for k in range(own):
+        sum_ref[:, k * LANES : (k + 1) * LANES] = back_ref[base + k, modes : 2 * modes, :]
+    stores = [pltpu.make_async_copy(sum_ref, sum_hbm, sems.at[slices])]
+    stores[0].start()
     for i in range(slices):
         pieces = []
         for chunk in range(i * width // LANES, (i + 1) * width // LANES):
@@ -250,10 +263,6 @@
             pltpu.make_async_copy(grad_ref.at[:, part], grad_hbm.at[0, :, part], sems.at[i])
         )
         stores[-1].start()
-    own = sum_ref.shape[1] // LANES
-    base = lax.axis_index("dp") * own
-    for k in range(own):
-        sum_ref[:, k * LANES : (k + 1) * LANES] = back_ref[base + k, modes : 2 * modes, :]
     for copy in stores:
         copy.wait()
 
@@ -300,7 +309,7 @@
     terms = pl.pallas_call(
         functools.partial(terms_kernel, 2, 256),
         in_specs=[anywhere] * 3,
-        out_specs=whole,
+        out_specs=anywhere,
         out_shape=jax.ShapeDtypeStruct((chunks, 3 * modes, LANES), jnp.float32),
         scratch_shapes=[
             pltpu.SMEM((modes,), jnp.float32),
@@ -310,6 +319,8 @@
             pltpu.VMEM((modes * rows // GROUP, 2 * rows), jnp.bfloat16),
             pltpu.VMEM((GROUP, modes, LANES), jnp.float32),
             pltpu.SemaphoreType.DMA((3, 2)),
+            pltpu.VMEM((chunks, 3 * modes, LANES), jnp.float32),
+            pltpu.SemaphoreType.DMA((2,)),
         ],
         compiler_params=params(FIRST_LIMIT),
         name="terms",
@@ -355,12 +366,16 @@
     return pl.pallas_call(
         functools.partial(finish_kernel, 4),
         in_specs=[whole] * 3,
-        out_specs=[anywhere, whole],
+        out_specs=[anywhere, anywhere],
         out_shape=[
             jax.ShapeDtypeStruct((1, rows, channels), jnp.bfloat16),
             jax.ShapeDtypeStruct((modes, channels // batch_count), jnp.float32),
         ],
-        scratch_shapes=[pltpu.VMEM((rows, channels), jnp.bfloat16), pltpu.SemaphoreType.DMA((4,))],
+        scratch_shapes=[
+            pltpu.VMEM((rows, channels), jnp.bfloat16),
+            pltpu.VMEM((modes, channels // batch_count), jnp.float32),
+            pltpu.SemaphoreType.DMA((5,)),
+        ],
         compiler_params=params(),
         name="finish",
     )(residues, local_grad, back)

time: 36.2 us -> 35.5 us (0.981)
  Pallas kernels: 8.72 us -> 8.08 us
    pallas_call x1, Pallas kernels: 1.81 us -> 1.21 us  [local(): pl.pallas_call(functools.partial(finish_kernel, 4), in_specs=[whole] * 3,...]
where the time goes in v5:
time: 35.5 us; the launch traced here: 35.2 us
  blocking collectives  9.74 us (27%)
  starting transfers between devices  8.95 us (25%)
  Pallas kernels  8.08 us (23%)
  waiting for transfers between devices  6.48 us (18%)
  local copies, waits for them, and re-layouts  1.23 us (3%)
  between operations  0.71 us (2%)
    all_to_all x1, blocking collectives, exchange(): return lax.all_to_all(slots, ('dp', 'seq'), 0, 0, axis_index_groups=groups)  9.74 us
    all_to_all x1, starting transfers between devices, exchange(): return lax.all_to_all(slots, ('dp', 'seq'), 0, 0, axis_index_groups=groups)  6.3 us
    pallas_call x1, Pallas kernels, local(): pl.pallas_call(functools.partial(terms_kernel, 2, 256), in_specs=[anywher...  3.48 us
    all_to_all x1, waiting for transfers between devices, exchange(): return lax.all_to_all(slots, ('dp', 'seq'), 0, 0, axis_index_groups=groups)  3.47 us
    pallas_call x1, Pallas kernels, local(): pl.pallas_call(functools.partial(local_grad_kernel, 512), in_specs=[anywh...  3.3 us
    ppermute x1, waiting for transfers between devices, local(): lax.ppermute(cross, 'seq', [(s, (s + half) % block_count) for s in range(...  3.01 us
    ppermute x1, starting transfers between devices, local(): lax.ppermute(cross, 'seq', [(s, (s + half) % block_count) for s in range(...  2.65 us
    unnamed x6, local copies, waits for them, and re-layouts  1.23 us
  transfers between devices with their start and end apart: 2, of which 2 were waited for; matrix products, arithmetic and copies ran while one was open for 0% of the time, Pallas kernels for 9%

profile of v5, /device:TPU:0, one launch (start us, length us, event | category | flops | bytes accessed | tf_op | source)
XLA Modules:
  0.0 35.2 jit_solution(15722290311629862563)
XLA Ops:
  0.6 0.0 copy-start.2
  0.6 0.0 copy-start.1
  0.7 3.5 %terms.1 = f32[32,24,128]{2,1,0:T(8,128)} custom-call(f32[8]{0:T(128)} %rates_hbm.3, bf16[1,128,4096]{2,1,0:T(8,128)(2,1)} %grad_hbm.3, bf16[1,128,4096]{2,1,0:T(8,128)(2,1)} %in_hbm.1), custom_call_target="tpu_custom_call" | custom-call | tf_op jit(solution)/shard_map/terms/pallas_call | solution.py:309
  4.1 6.3 %all-to-all-start = ((f32[16,48,128]{2,1,0:T(8,128)}), f32[16,48,128]{2,1,0:T(8,128)S(1)}, u32[]{:S(2)}, u32[]{:S(2)}) async-start(f32[16,48,128]{2,1,0:T(8,128)} %bitcast.8), calls=%async_computation | async-start | bytes 786432 | tf_op jit(solution)/shard_map/all_to_all | solution.py:305
  10.4 0.0 copy-done.2
  10.5 0.0 copy-done.1
  10.5 0.0 copy-start
  10.5 1.2 %copy-done = bf16[1,128,4096]{2,1,0:T(8,128)(2,1)S(1)} copy-done((bf16[1,128,4096]{2,1,0:T(8,128)(2,1)S(1)}, bf16[1,128,4096]{2,1,0:T(8,128)(2,1)}, u32[]{:S(2)}) %copy-start) | copy-done | bytes 1048600
  11.7 3.3 %local_grad.1.local_ref = f32[128,4352]{1,0:T(8,128)S(1)} custom-call(f32[8]{0:T(128)S(1)} %copy-done.2, f32[8,4096]{1,0:T(8,128)S(1)} %copy-done.1, bf16[1,128,4096]{2,1,0:T(8,128)(2,1)S(1)} %copy-done), custom_call_target="tpu_custom_call" | custom-call | flops 1073741824 | bytes 3145728 | tf_op jit(solution)/shard_map/local_grad/pallas_call | solution.py:329
  15.0 3.5 %all-to-all-done = f32[16,48,128]{2,1,0:T(8,128)S(1)} async-done(((f32[16,48,128]{2,1,0:T(8,128)}), f32[16,48,128]{2,1,0:T(8,128)S(1)}, u32[]{:S(2)}, u32[]{:S(2)}) %all-to-all-start) | async-done | bytes 393248 | tf_op jit(solution)/shard_map/all_to_all | solution.py:305
  18.5 2.7 %collective-permute-start = (f32[10,8,128]{2,1,0:T(8,128)S(1)}, f32[10,8,128]{2,1,0:T(8,128)S(1)}, u32[]{:S(2)}, u32[]{:S(2)}) collective-permute-start(f32[10,8,128]{2,1,0:T(8,128)S(1)} %half.1.own_ref), channel_id=1, source_target_pairs={{0,4},{1,5},{2,6},{3,7},{4,0},{5,1},{6,2},{7,3},{8,12},{9,13},{10,... | collective-permute-start | bytes 122888 | tf_op jit(solution)/shard_map/ppermute | solution.py:356
  21.2 3.0 %collective-permute-done.other_ref = f32[10,8,128]{2,1,0:T(8,128)S(1)} collective-permute-done((f32[10,8,128]{2,1,0:T(8,128)S(1)}, f32[10,8,128]{2,1,0:T(8,128)S(1)}, u32[]{:S(2)}, u32[]{:S(2)}) %collective-permute-start) | collective-permute-done | bytes 40992 | tf_op jit(solution)/shard_map/ppermute | solution.py:356
  24.2 9.7 %all_to_all.10 = f32[16,32,128]{2,1,0:T(8,128)S(1)} all-to-all(f32[16,32,128]{2,1,0:T(8,128)S(1)} %bitcast.7), channel_id=1, replica_groups={{0,1,2,3,8,9,10,11,16,17,18,19,24,25,26,27},{4,5,6,7,12,13,14,15,20,21,..., dimensions={0} | all-to-all | bytes 524288 | tf_op jit(solution)/shard_map/all_to_all | solution.py:305
  34.0 1.2 %finish.1 = (bf16[1,128,4096]{2,1,0:T(8,128)(2,1)}, f32[8,1024]{1,0:T(8,128)}) custom-call(f32[8,4096]{1,0:T(8,128)S(1)} %copy-done.1, f32[128,4352]{1,0:T(8,128)S(1)} %local_grad.1.local_ref, f32[32,16,128]{2,1,0:T(8,128)S(1)} %bitcast.6), custom_call_target="tpu_custom_call" | custom-call | tf_op jit(solution)/shard_map/finish/pallas_call | solution.py:366
  (2 shorter events, 0.1 us)
Async XLA Ops:
  0.6 9.8 %copy-start.2 = (f32[8]{0:T(128)S(1)}, f32[8]{0:T(128)}, u32[]{:S(2)}) copy-start(f32[8]{0:T(128)} %rates_hbm.3) | copy-start | bytes 100
  0.6 9.8 %copy-start.1 = (f32[8,4096]{1,0:T(8,128)S(1)}, f32[8,4096]{1,0:T(8,128)}, u32[]{:S(2)}) copy-start(f32[8,4096]{1,0:T(8,128)} %residues_ref.3) | copy-start | bytes 393220
  4.1 14.3 %all-to-all-start = ((f32[16,48,128]{2,1,0:T(8,128)}), f32[16,48,128]{2,1,0:T(8,128)S(1)}, u32[]{:S(2)}, u32[]{:S(2)}) async-start(f32[16,48,128]{2,1,0:T(8,128)} %bitcast.8), calls=%async_computation | async-start | bytes 786432 | tf_op jit(solution)/shard_map/all_to_all | solution.py:305
  10.5 1.2 %copy-start = (bf16[1,128,4096]{2,1,0:T(8,128)(2,1)S(1)}, bf16[1,128,4096]{2,1,0:T(8,128)(2,1)}, u32[]{:S(2)}) copy-start(bf16[1,128,4096]{2,1,0:T(8,128)(2,1)} %grad_hbm.3) | copy-start | bytes 3145732
  18.5 5.7 %collective-permute-start = (f32[10,8,128]{2,1,0:T(8,128)S(1)}, f32[10,8,128]{2,1,0:T(8,128)S(1)}, u32[]{:S(2)}, u32[]{:S(2)}) collective-permute-start(f32[10,8,128]{2,1,0:T(8,128)S(1)} %half.1.own_ref), channel_id=1, source_target_pairs={{0,4},{1,5},{2,6},{3,7},{4,0},{5,1},{6,2},{7,3},{8,12},{9,13},{10,... | collective-permute-start | bytes 122888 | tf_op jit(solution)/shard_map/ppermute | solution.py:356

commit v6 on v5

--- a/solution.py
+++ b/solution.py
@@ -44,6 +44,7 @@
 def terms_kernel(
     slices,
     sub,
+    slot,
     rates_hbm,
     grad_hbm,
     in_hbm,
@@ -128,11 +129,12 @@
                 local = local + weight * jnp.sum(product, axis=0, keepdims=True)
             for k in range(sub // LANES):
                 lanes = slice(k * LANES, (k + 1) * LANES)
-                chunk = first // LANES + k
+                chunk = slot(first // LANES + k)
                 stage_ref[chunk, 0:modes, :] = state[:, lanes]
                 stage_ref[chunk, modes : 2 * modes, :] = carry[:, lanes]
                 stage_ref[chunk, 2 * modes : 3 * modes, :] = local[:, lanes]
-        span = pl.ds(i * width // LANES, width // LANES)
+        chunks = [slot(chunk) for chunk in range(i * width // LANES, (i + 1) * width // LANES)]
+        span = pl.ds(min(chunks), len(chunks))
         stores.append(pltpu.make_async_copy(stage_ref.at[span], out_ref.at[span], out_sems.at[i]))
         stores[-1].start()
     for copy in stores:
@@ -181,7 +183,7 @@
     return lax.fori_loop(0, count, body, start, unroll=count <= 8)
 
 
-def half_kernel(batch_count, half, local_ref, terms_ref, out_ref):
+def half_kernel(batch_count, half, mask, local_ref, terms_ref, out_ref):
     modes, width = out_ref.shape[1:]
     pieces = terms_ref.shape[0] // (batch_count * half)
     decay = block_decay(local_ref, modes, width)
@@ -192,13 +194,13 @@
         def sequence(b, total):
             def state(j, pair):
                 total, incoming = pair
-                at = (b * half + half - 1 - j) * pieces + k
+                at = ((b * half + half - 1 - j) ^ mask) * pieces + k
                 weights = terms_ref[at, modes : 2 * modes, :]
                 total = total + (terms_ref[at, 2 * modes : 3 * modes, :] + incoming * weights)
                 return total, terms_ref[at, 0:modes, :] + decay * incoming
 
             def weight(j, before):
-                return terms_ref[(b * half + j) * pieces + k, modes : 2 * modes, :] + decay * before
+                return terms_ref[((b * half + j) ^ mask) * pieces + k, modes : 2 * modes, :] + decay * before
 
             total, incoming = steps(half, state, (total, zero))
             out_ref[b * pieces + k] = jnp.where(later, incoming, steps(half, weight, zero))
@@ -207,7 +209,7 @@
         out_ref[batch_count * pieces + k] = steps(batch_count, sequence, zero)
 
 
-def scan_kernel(batch_count, half, local_ref, terms_ref, own_ref, other_ref, out_ref):
+def scan_kernel(batch_count, half, mask, local_ref, terms_ref, own_ref, other_ref, out_ref):
     modes, width = own_ref.shape[1:]
     pieces = terms_ref.shape[0] // (batch_count * half)
     decay = block_decay(local_ref, modes, width)
@@ -220,7 +222,7 @@
             other = other_ref[b * pieces + k]
 
             def block(j, incoming):
-                at = (b * half + half - 1 - j) * pieces + k
+                at = ((b * half + half - 1 - j) ^ mask) * pieces + k
                 out_ref[at, 0:modes, :] = incoming
                 return terms_ref[at, 0:modes, :] + decay * incoming
 
@@ -236,7 +238,7 @@
         lax.fori_loop(0, batch_count * half, spread, 0, unroll=8)
 
 
-def finish_kernel(slices, residues_ref, local_ref, back_ref, grad_hbm, sum_hbm, grad_ref, sum_ref, sems):
+def finish_kernel(slices, slot, residues_ref, local_ref, back_ref, grad_hbm, sum_hbm, grad_ref, sum_ref, sems):
     modes, channels = residues_ref.shape
     rows = local_ref.shape[0]
     width = channels // slices
@@ -244,14 +246,14 @@
     own = sum_ref.shape[1] // LANES
     base = lax.axis_index("dp") * own
     for k in range(own):
-        sum_ref[:, k * LANES : (k + 1) * LANES] = back_ref[base + k, modes : 2 * modes, :]
+        sum_ref[:, k * LANES : (k + 1) * LANES] = back_ref[slot(base + k), modes : 2 * modes, :]
     stores = [pltpu.make_async_copy(sum_ref, sum_hbm, sems.at[slices])]
     stores[0].start()
     for i in range(slices):
         pieces = []
         for chunk in range(i * width // LANES, (i + 1) * width // LANES):
             lanes = slice(chunk * LANES, (chunk + 1) * LANES)
-            value = residues_ref[:, lanes] * back_ref[chunk, 0:modes, :]
+            value = residues_ref[:, lanes] * back_ref[slot(chunk), 0:modes, :]
             high = value.astype(jnp.bfloat16).astype(jnp.float32)
             pieces.append(jnp.concatenate([high, value - high], axis=0).astype(jnp.bfloat16))
         carried = jnp.dot(
@@ -296,18 +298,28 @@
     chunks = channels // LANES
     width = min(LANES, channels // owners)
     pieces = channels // (owners * width)
-    groups = [
-        [d * block_count + first + j for d in range(batch_count) for j in range(half)]
-        for first in (0, half)
-    ]
-
-    def exchange(slots):
-        return lax.all_to_all(slots, ("dp", "seq"), 0, 0, axis_index_groups=groups)
-
     anywhere = pl.BlockSpec(memory_space=pl.ANY)
     whole = pl.BlockSpec(memory_space=pltpu.VMEM)
+    mask = (batch_count - 1) * half + 1 if half > 1 and owners & (owners - 1) == 0 else 0
+
+    def exchange(slots):
+        places = [d * block_count + j for d in range(batch_count) for j in range(half)]
+        groups = [[first + places[p ^ mask] for p in range(owners)] for first in (0, half)]
+        return lax.all_to_all(slots, ("dp", "seq"), 0, 0, axis_index_groups=groups)
+
+    def slot(chunk):
+        if owners > chunks:
+            return chunk
+        share = chunks // owners
+        return ((chunk // share) ^ mask) * share + chunk % share
+
+    def reorder(slots):
+        if owners <= chunks:
+            return slots
+        return slots[jnp.array([p ^ mask for p in range(owners)])]
+
     terms = pl.pallas_call(
-        functools.partial(terms_kernel, 2, 256),
+        functools.partial(terms_kernel, 2, 256, slot),
         in_specs=[anywhere] * 3,
         out_specs=anywhere,
         out_shape=jax.ShapeDtypeStruct((chunks, 3 * modes, LANES), jnp.float32),
@@ -325,7 +337,8 @@
         compiler_params=params(FIRST_LIMIT),
         name="terms",
     )(decay_rates, grad_out, block_in)
-    terms = exchange(to_owners(terms, owners)).reshape(owners * pieces, 3 * modes, width)
+    terms = exchange(reorder(to_owners(terms, owners)))
+    terms = terms.reshape(owners * pieces, 3 * modes, width)
     local_grad = pl.pallas_call(
         functools.partial(local_grad_kernel, 512),
         in_specs=[anywhere, whole, anywhere],
@@ -346,7 +359,7 @@
         name="local_grad",
     )(decay_rates, residues, grad_out)
     cross = pl.pallas_call(
-        functools.partial(half_kernel, batch_count, half),
+        functools.partial(half_kernel, batch_count, half, mask),
         in_specs=[whole, whole],
         out_specs=whole,
         out_shape=jax.ShapeDtypeStruct(((batch_count + 1) * pieces, modes, width), jnp.float32),
@@ -355,16 +368,17 @@
     )(local_grad, terms)
     other = lax.ppermute(cross, "seq", [(s, (s + half) % block_count) for s in range(block_count)])
     back = pl.pallas_call(
-        functools.partial(scan_kernel, batch_count, half),
+        functools.partial(scan_kernel, batch_count, half, mask),
         in_specs=[whole] * 4,
         out_specs=whole,
         out_shape=jax.ShapeDtypeStruct((owners * pieces, 2 * modes, width), jnp.float32),
         compiler_params=params(),
         name="scan",
     )(local_grad, terms, cross, other)
-    back = from_owners(exchange(back.reshape(owners, pieces * 2 * modes, width)), chunks)
+    back = exchange(back.reshape(owners, pieces * 2 * modes, width))
+    back = from_owners(reorder(back), chunks)
     return pl.pallas_call(
-        functools.partial(finish_kernel, 4),
+        functools.partial(finish_kernel, 4, slot),
         in_specs=[whole] * 3,
         out_specs=[anywhere, anywhere],
         out_shape=[

time: 35.5 us -> 33.5 us (0.944)
  waiting for transfers between devices: 6.48 us -> 4.77 us
  blocking collectives: 9.74 us -> 8.99 us
  starting transfers between devices: 8.95 us -> 9.44 us
    all_to_all x1, waiting for transfers between devices: 3.47 us -> 2 us  [exchange(): return lax.all_to_all(slots, ('dp', 'seq'), 0, 0, axis_index_groups=groups)]
    all_to_all x1, blocking collectives: 9.74 us -> 8.99 us  [exchange(): return lax.all_to_all(slots, ('dp', 'seq'), 0, 0, axis_index_groups=groups)]
    all_to_all x1, starting transfers between devices: 6.3 us -> 6.78 us  [exchange(): return lax.all_to_all(slots, ('dp', 'seq'), 0, 0, axis_index_groups=groups)]
  transfers between devices with their start and end apart: 2 -> 2, of which waited for: 2 -> 2; matrix products, arithmetic and copies ran while one was open for 0% -> 0% of each run, Pallas kernels for 9% -> 10%
where the time goes in v6:
time: 33.5 us; the launch traced here: 33.2 us
  starting transfers between devices  9.44 us (28%)
  blocking collectives  8.99 us (27%)
  Pallas kernels  8.06 us (24%)
  waiting for transfers between devices  4.77 us (14%)
  local copies, waits for them, and re-layouts  1.23 us (4%)
  between operations  0.69 us (2%)
    all_to_all x1, blocking collectives, exchange(): return lax.all_to_all(slots, ('dp', 'seq'), 0, 0, axis_index_groups=groups)  8.99 us
    all_to_all x1, starting transfers between devices, exchange(): return lax.all_to_all(slots, ('dp', 'seq'), 0, 0, axis_index_groups=groups)  6.78 us
    pallas_call x1, Pallas kernels, local(): pl.pallas_call(functools.partial(terms_kernel, 2, 256, slot), in_specs=[a...  3.48 us
    pallas_call x1, Pallas kernels, local(): pl.pallas_call(functools.partial(local_grad_kernel, 512), in_specs=[anywh...  3.29 us
    ppermute x1, waiting for transfers between devices, local(): lax.ppermute(cross, 'seq', [(s, (s + half) % block_count) for s in range(...  2.77 us
    ppermute x1, starting transfers between devices, local(): lax.ppermute(cross, 'seq', [(s, (s + half) % block_count) for s in range(...  2.66 us
    all_to_all x1, waiting for transfers between devices, exchange(): return lax.all_to_all(slots, ('dp', 'seq'), 0, 0, axis_index_groups=groups)  2 us
    unnamed x6, local copies, waits for them, and re-layouts  1.23 us
  transfers between devices with their start and end apart: 2, of which 2 were waited for; matrix products, arithmetic and copies ran while one was open for 0% of the time, Pallas kernels for 10%

profile of v6, /device:TPU:0, one launch (start us, length us, event | category | flops | bytes accessed | tf_op | source)
XLA Modules:
  0.0 33.2 jit_solution(69333090482450949)
XLA Ops:
  0.6 0.0 copy-start.2
  0.6 0.0 copy-start.1
  0.7 3.5 %terms.1 = f32[32,24,128]{2,1,0:T(8,128)} custom-call(f32[8]{0:T(128)} %rates_hbm.3, bf16[1,128,4096]{2,1,0:T(8,128)(2,1)} %grad_hbm.3, bf16[1,128,4096]{2,1,0:T(8,128)(2,1)} %in_hbm.1), custom_call_target="tpu_custom_call" | custom-call | tf_op jit(solution)/shard_map/terms/pallas_call | solution.py:321
  4.1 6.8 %all-to-all-start = ((f32[16,48,128]{2,1,0:T(8,128)}), f32[16,48,128]{2,1,0:T(8,128)S(1)}, u32[]{:S(2)}, u32[]{:S(2)}) async-start(f32[16,48,128]{2,1,0:T(8,128)} %bitcast.8), calls=%async_computation | async-start | bytes 786432 | tf_op jit(solution)/shard_map/all_to_all | solution.py:308
  10.9 0.0 copy-done.2
  10.9 0.0 copy-done.1
  10.9 0.0 copy-start
  11.0 1.2 %copy-done = bf16[1,128,4096]{2,1,0:T(8,128)(2,1)S(1)} copy-done((bf16[1,128,4096]{2,1,0:T(8,128)(2,1)S(1)}, bf16[1,128,4096]{2,1,0:T(8,128)(2,1)}, u32[]{:S(2)}) %copy-start) | copy-done | bytes 1048600
  12.2 3.3 %local_grad.1.local_ref = f32[128,4352]{1,0:T(8,128)S(1)} custom-call(f32[8]{0:T(128)S(1)} %copy-done.2, f32[8,4096]{1,0:T(8,128)S(1)} %copy-done.1, bf16[1,128,4096]{2,1,0:T(8,128)(2,1)S(1)} %copy-done), custom_call_target="tpu_custom_call" | custom-call | flops 1073741824 | bytes 3145728 | tf_op jit(solution)/shard_map/local_grad/pallas_call | solution.py:342
  15.5 2.0 %all-to-all-done = f32[16,48,128]{2,1,0:T(8,128)S(1)} async-done(((f32[16,48,128]{2,1,0:T(8,128)}), f32[16,48,128]{2,1,0:T(8,128)S(1)}, u32[]{:S(2)}, u32[]{:S(2)}) %all-to-all-start) | async-done | bytes 393248 | tf_op jit(solution)/shard_map/all_to_all | solution.py:308
  17.5 2.7 %collective-permute-start = (f32[10,8,128]{2,1,0:T(8,128)S(1)}, f32[10,8,128]{2,1,0:T(8,128)S(1)}, u32[]{:S(2)}, u32[]{:S(2)}) collective-permute-start(f32[10,8,128]{2,1,0:T(8,128)S(1)} %half.1.own_ref), channel_id=1, source_target_pairs={{0,4},{1,5},{2,6},{3,7},{4,0},{5,1},{6,2},{7,3},{8,12},{9,13},{10,... | collective-permute-start | bytes 122888 | tf_op jit(solution)/shard_map/ppermute | solution.py:369
  20.2 2.8 %collective-permute-done.other_ref = f32[10,8,128]{2,1,0:T(8,128)S(1)} collective-permute-done((f32[10,8,128]{2,1,0:T(8,128)S(1)}, f32[10,8,128]{2,1,0:T(8,128)S(1)}, u32[]{:S(2)}, u32[]{:S(2)}) %collective-permute-start) | collective-permute-done | bytes 40992 | tf_op jit(solution)/shard_map/ppermute | solution.py:369
  23.0 9.0 %all_to_all.10 = f32[16,32,128]{2,1,0:T(8,128)S(1)} all-to-all(f32[16,32,128]{2,1,0:T(8,128)S(1)} %bitcast.7), channel_id=1, replica_groups={{25,24,27,26,17,16,19,18,9,8,11,10,1,0,3,2},{29,28,31,30,21,20,23,22,13..., dimensions={0} | all-to-all | bytes 524288 | tf_op jit(solution)/shard_map/all_to_all | solution.py:308
  32.0 1.2 %finish.1 = (bf16[1,128,4096]{2,1,0:T(8,128)(2,1)}, f32[8,1024]{1,0:T(8,128)}) custom-call(f32[8,4096]{1,0:T(8,128)S(1)} %copy-done.1, f32[128,4352]{1,0:T(8,128)S(1)} %local_grad.1.local_ref, f32[32,16,128]{2,1,0:T(8,128)S(1)} %bitcast.6), custom_call_target="tpu_custom_call" | custom-call | tf_op jit(solution)/shard_map/finish/pallas_call | solution.py:380
  (2 shorter events, 0.1 us)
Async XLA Ops:
  0.6 10.3 %copy-start.2 = (f32[8]{0:T(128)S(1)}, f32[8]{0:T(128)}, u32[]{:S(2)}) copy-start(f32[8]{0:T(128)} %rates_hbm.3) | copy-start | bytes 100
  0.6 10.3 %copy-start.1 = (f32[8,4096]{1,0:T(8,128)S(1)}, f32[8,4096]{1,0:T(8,128)}, u32[]{:S(2)}) copy-start(f32[8,4096]{1,0:T(8,128)} %residues_ref.3) | copy-start | bytes 393220
  4.1 13.3 %all-to-all-start = ((f32[16,48,128]{2,1,0:T(8,128)}), f32[16,48,128]{2,1,0:T(8,128)S(1)}, u32[]{:S(2)}, u32[]{:S(2)}) async-start(f32[16,48,128]{2,1,0:T(8,128)} %bitcast.8), calls=%async_computation | async-start | bytes 786432 | tf_op jit(solution)/shard_map/all_to_all | solution.py:308
  10.9 1.2 %copy-start = (bf16[1,128,4096]{2,1,0:T(8,128)(2,1)S(1)}, bf16[1,128,4096]{2,1,0:T(8,128)(2,1)}, u32[]{:S(2)}) copy-start(bf16[1,128,4096]{2,1,0:T(8,128)(2,1)} %grad_hbm.3) | copy-start | bytes 3145732
  17.5 5.4 %collective-permute-start = (f32[10,8,128]{2,1,0:T(8,128)S(1)}, f32[10,8,128]{2,1,0:T(8,128)S(1)}, u32[]{:S(2)}, u32[]{:S(2)}) collective-permute-start(f32[10,8,128]{2,1,0:T(8,128)S(1)} %half.1.own_ref), channel_id=1, source_target_pairs={{0,4},{1,5},{2,6},{3,7},{4,0},{5,1},{6,2},{7,3},{8,12},{9,13},{10,... | collective-permute-start | bytes 122888 | tf_op jit(solution)/shard_map/ppermute | solution.py:369

commit v7 on v6

--- a/solution.py
+++ b/solution.py
@@ -44,7 +44,7 @@
 def terms_kernel(
     slices,
     sub,
-    slot,
+    places,
     rates_hbm,
     grad_hbm,
     in_hbm,
@@ -128,13 +128,15 @@
                 weight = jnp.concatenate([lag_ref[k]] * (sub // LANES), axis=1)
                 local = local + weight * jnp.sum(product, axis=0, keepdims=True)
             for k in range(sub // LANES):
-                lanes = slice(k * LANES, (k + 1) * LANES)
-                chunk = slot(first // LANES + k)
-                stage_ref[chunk, 0:modes, :] = state[:, lanes]
-                stage_ref[chunk, modes : 2 * modes, :] = carry[:, lanes]
-                stage_ref[chunk, 2 * modes : 3 * modes, :] = local[:, lanes]
-        chunks = [slot(chunk) for chunk in range(i * width // LANES, (i + 1) * width // LANES)]
-        span = pl.ds(min(chunks), len(chunks))
+                for low, high, at in places(first // LANES + k):
+                    lanes = slice(k * LANES + low, k * LANES + high)
+                    stage_ref[at + (slice(0, modes), slice(low, high))] = state[:, lanes]
+                    stage_ref[at + (slice(modes, 2 * modes), slice(low, high))] = carry[:, lanes]
+                    stage_ref[at + (slice(2 * modes, 3 * modes), slice(low, high))] = local[:, lanes]
+        chunks = range(i * width // LANES, (i + 1) * width // LANES)
+        used = sorted({at for chunk in chunks for _, _, at in places(chunk)})
+        slots, pieces = sorted({at[0] for at in used}), sorted({at[1] for at in used})
+        span = (pl.ds(slots[0], len(slots)), pl.ds(pieces[0], len(pieces)))
         stores.append(pltpu.make_async_copy(stage_ref.at[span], out_ref.at[span], out_sems.at[i]))
         stores[-1].start()
     for copy in stores:
@@ -209,11 +211,12 @@
         out_ref[batch_count * pieces + k] = steps(batch_count, sequence, zero)
 
 
-def scan_kernel(batch_count, half, mask, local_ref, terms_ref, own_ref, other_ref, out_ref):
+def scan_kernel(batch_count, half, mask, paired, local_ref, terms_ref, own_ref, other_ref, out_ref):
     modes, width = own_ref.shape[1:]
     pieces = terms_ref.shape[0] // (batch_count * half)
     decay = block_decay(local_ref, modes, width)
     later = lax.axis_index("seq") >= half
+    totals = []
     for k in range(pieces):
         last = batch_count * pieces + k
         total = own_ref[last] + other_ref[last]
@@ -222,38 +225,41 @@
             other = other_ref[b * pieces + k]
 
             def block(j, incoming):
-                at = ((b * half + half - 1 - j) ^ mask) * pieces + k
-                out_ref[at, 0:modes, :] = incoming
-                return terms_ref[at, 0:modes, :] + decay * incoming
+                at = (b * half + half - 1 - j) ^ mask
+                out_ref[at, k * modes : (k + 1) * modes, :] = incoming
+                return terms_ref[at * pieces + k, 0:modes, :] + decay * incoming
 
             steps(half, block, jnp.where(later, 0.0, other))
             return total + own_ref[b * pieces + k] * other
 
-        total = steps(batch_count, sequence, total)
-
-        def spread(i, carry):
-            out_ref[i * pieces + k, modes : 2 * modes, :] = total
+        totals.append(steps(batch_count, sequence, total))
+    if paired:
+        for at in range(batch_count * half):
+            out_ref[at ^ mask, pieces * modes :, :] = totals[at // half // 2]
+    else:
+
+        def spread(at, carry):
+            out_ref[at, pieces * modes :, :] = jnp.concatenate(totals, axis=0)
             return carry
 
         lax.fori_loop(0, batch_count * half, spread, 0, unroll=8)
 
 
-def finish_kernel(slices, slot, residues_ref, local_ref, back_ref, grad_hbm, sum_hbm, grad_ref, sum_ref, sems):
+def finish_kernel(slices, read_incoming, read_total, residues_ref, local_ref, back_ref, grad_hbm, sum_hbm, grad_ref, sum_ref, sems):
     modes, channels = residues_ref.shape
     rows = local_ref.shape[0]
     width = channels // slices
     carry = local_ref[:, channels : channels + 2 * modes].astype(jnp.bfloat16)
     own = sum_ref.shape[1] // LANES
-    base = lax.axis_index("dp") * own
     for k in range(own):
-        sum_ref[:, k * LANES : (k + 1) * LANES] = back_ref[slot(base + k), modes : 2 * modes, :]
+        sum_ref[:, k * LANES : (k + 1) * LANES] = read_total(back_ref, k)
     stores = [pltpu.make_async_copy(sum_ref, sum_hbm, sems.at[slices])]
     stores[0].start()
     for i in range(slices):
         pieces = []
         for chunk in range(i * width // LANES, (i + 1) * width // LANES):
             lanes = slice(chunk * LANES, (chunk + 1) * LANES)
-            value = residues_ref[:, lanes] * back_ref[slot(chunk), 0:modes, :]
+            value = residues_ref[:, lanes] * read_incoming(back_ref, chunk)
             high = value.astype(jnp.bfloat16).astype(jnp.float32)
             pieces.append(jnp.concatenate([high, value - high], axis=0).astype(jnp.bfloat16))
         carried = jnp.dot(
@@ -270,9 +276,9 @@
 
 
 def to_owners(chunks, owners):
-    count, rows, lanes = chunks.shape
-    if owners <= count:
-        return chunks.reshape(owners, count // owners * rows, lanes)
+    count, pieces, rows, lanes = chunks.shape
+    if owners == count:
+        return chunks.reshape(owners, pieces * rows, lanes)
     narrow = count * lanes // owners
     parts = chunks.reshape(count, rows, lanes // narrow, narrow)
     return jnp.swapaxes(parts, 1, 2).reshape(owners, rows, narrow)
@@ -281,7 +287,7 @@
 def from_owners(parts, count):
     owners, rows, narrow = parts.shape
     if owners <= count:
-        return parts.reshape(count, owners * rows // count, narrow)
+        return parts
     chunks = parts.reshape(count, owners // count, rows, narrow)
     return jnp.swapaxes(chunks, 1, 2).reshape(count, rows, LANES)
 
@@ -307,11 +313,40 @@
         groups = [[first + places[p ^ mask] for p in range(owners)] for first in (0, half)]
         return lax.all_to_all(slots, ("dp", "seq"), 0, 0, axis_index_groups=groups)
 
-    def slot(chunk):
-        if owners > chunks:
-            return chunk
-        share = chunks // owners
-        return ((chunk // share) ^ mask) * share + chunk % share
+    slot_count = min(owners, chunks)
+    own = chunks // batch_count
+    paired = slot_count == 2 * own and pieces * 2 == batch_count
+    total_rows = modes if paired else pieces * modes
+    if owners > chunks:
+        slot = lambda owner: owner
+    else:
+        slot = lambda owner: owner ^ mask
+
+    def places(chunk):
+        if not paired:
+            return [(0, LANES, (slot(chunk // pieces), chunk % pieces))]
+        d, m = chunk // own, chunk % own
+        low, high = slot(2 * m + d % 2), slot(2 * m + 1 - d % 2)
+        return [(0, LANES // 2, (low, d // 2)), (LANES // 2, LANES, (high, d // 2))]
+
+    def in_low_half():
+        return lax.broadcasted_iota(jnp.int32, (modes, LANES), 1) < LANES // 2
+
+    def read_incoming(back_ref, chunk):
+        parts = [
+            back_ref[at, piece * modes : (piece + 1) * modes, :] for _, _, (at, piece) in places(chunk)
+        ]
+        return jnp.where(in_low_half(), *parts) if paired else parts[0]
+
+    def read_total(back_ref, m):
+        d = lax.axis_index("dp")
+        if paired:
+            first = back_ref[slot(2 * m), pieces * modes :, :]
+            second = back_ref[slot(2 * m + 1), pieces * modes :, :]
+            return jnp.where(in_low_half() == (d % 2 == 0), first, second)
+        chunk = d * own + m
+        row = pl.multiple_of((pieces + chunk % pieces) * modes, modes)
+        return back_ref[slot(chunk // pieces), pl.ds(row, modes), :]
 
     def reorder(slots):
         if owners <= chunks:
@@ -319,10 +354,10 @@
         return slots[jnp.array([p ^ mask for p in range(owners)])]
 
     terms = pl.pallas_call(
-        functools.partial(terms_kernel, 2, 256, slot),
+        functools.partial(terms_kernel, 2, 256, places),
         in_specs=[anywhere] * 3,
         out_specs=anywhere,
-        out_shape=jax.ShapeDtypeStruct((chunks, 3 * modes, LANES), jnp.float32),
+        out_shape=jax.ShapeDtypeStruct((slot_count, pieces, 3 * modes, LANES), jnp.float32),
         scratch_shapes=[
             pltpu.SMEM((modes,), jnp.float32),
             pltpu.VMEM((rows, channels), jnp.bfloat16),
@@ -331,7 +366,7 @@
             pltpu.VMEM((modes * rows // GROUP, 2 * rows), jnp.bfloat16),
             pltpu.VMEM((GROUP, modes, LANES), jnp.float32),
             pltpu.SemaphoreType.DMA((3, 2)),
-            pltpu.VMEM((chunks, 3 * modes, LANES), jnp.float32),
+            pltpu.VMEM((slot_count, pieces, 3 * modes, LANES), jnp.float32),
             pltpu.SemaphoreType.DMA((2,)),
         ],
         compiler_params=params(FIRST_LIMIT),
@@ -368,17 +403,16 @@
     )(local_grad, terms)
     other = lax.ppermute(cross, "seq", [(s, (s + half) % block_count) for s in range(block_count)])
     back = pl.pallas_call(
-        functools.partial(scan_kernel, batch_count, half, mask),
+        functools.partial(scan_kernel, batch_count, half, mask, paired),
         in_specs=[whole] * 4,
         out_specs=whole,
-        out_shape=jax.ShapeDtypeStruct((owners * pieces, 2 * modes, width), jnp.float32),
+        out_shape=jax.ShapeDtypeStruct((owners, pieces * modes + total_rows, width), jnp.float32),
         compiler_params=params(),
         name="scan",
     )(local_grad, terms, cross, other)
-    back = exchange(back.reshape(owners, pieces * 2 * modes, width))
-    back = from_owners(reorder(back), chunks)
+    back = from_owners(reorder(exchange(back)), chunks)
     return pl.pallas_call(
-        functools.partial(finish_kernel, 4, slot),
+        functools.partial(finish_kernel, 4, read_incoming, read_total),
         in_specs=[whole] * 3,
         out_specs=[anywhere, anywhere],
         out_shape=[

time: 33.5 us -> 32.8 us (0.979)
  blocking collectives: 8.99 us -> 8.33 us
    all_to_all x1, blocking collectives: 8.99 us -> 8.33 us  [exchange(): return lax.all_to_all(slots, ('dp', 'seq'), 0, 0, axis_index_groups=groups)]
where the time goes in v7:
time: 32.8 us; the launch traced here: 32.5 us
  starting transfers between devices  9.44 us (29%)
  blocking collectives  8.33 us (25%)
  Pallas kernels  8.06 us (25%)
  waiting for transfers between devices  4.75 us (14%)
  local copies, waits for them, and re-layouts  1.23 us (4%)
  between operations  0.69 us (2%)
    all_to_all x1, blocking collectives, exchange(): return lax.all_to_all(slots, ('dp', 'seq'), 0, 0, axis_index_groups=groups)  8.33 us
    all_to_all x1, starting transfers between devices, exchange(): return lax.all_to_all(slots, ('dp', 'seq'), 0, 0, axis_index_groups=groups)  6.77 us
    pallas_call x1, Pallas kernels, local(): pl.pallas_call(functools.partial(terms_kernel, 2, 256, places), in_specs=...  3.48 us
    pallas_call x1, Pallas kernels, local(): pl.pallas_call(functools.partial(local_grad_kernel, 512), in_specs=[anywh...  3.3 us
    ppermute x1, waiting for transfers between devices, local(): lax.ppermute(cross, 'seq', [(s, (s + half) % block_count) for s in range(...  2.76 us
    ppermute x1, starting transfers between devices, local(): lax.ppermute(cross, 'seq', [(s, (s + half) % block_count) for s in range(...  2.67 us
    all_to_all x1, waiting for transfers between devices, exchange(): return lax.all_to_all(slots, ('dp', 'seq'), 0, 0, axis_index_groups=groups)  1.99 us
    unnamed x6, local copies, waits for them, and re-layouts  1.23 us
  transfers between devices with their start and end apart: 2, of which 2 were waited for; matrix products, arithmetic and copies ran while one was open for 0% of the time, Pallas kernels for 10%

profile of v7, /device:TPU:0, one launch (start us, length us, event | category | flops | bytes accessed | tf_op | source)
XLA Modules:
  0.0 32.5 jit_solution(14702664338729642330)
XLA Ops:
  0.6 0.0 copy-start.2
  0.6 0.0 copy-start.1
  0.7 3.5 %terms.1 = f32[16,2,24,128]{3,2,1,0:T(8,128)} custom-call(f32[8]{0:T(128)} %rates_hbm.3, bf16[1,128,4096]{2,1,0:T(8,128)(2,1)} %grad_hbm.3, bf16[1,128,4096]{2,1,0:T(8,128)(2,1)} %in_hbm.1), custom_call_target="tpu_custom_call" | custom-call | tf_op jit(solution)/shard_map/terms/pallas_call | solution.py:356
  4.1 6.8 %all-to-all-start = ((f32[16,48,128]{2,1,0:T(8,128)}), f32[16,48,128]{2,1,0:T(8,128)S(1)}, u32[]{:S(2)}, u32[]{:S(2)}) async-start(f32[16,48,128]{2,1,0:T(8,128)} %bitcast.4), calls=%async_computation | async-start | bytes 786432 | tf_op jit(solution)/shard_map/all_to_all | solution.py:314
  10.9 0.0 copy-done.2
  10.9 0.0 copy-done.1
  10.9 0.0 copy-start
  10.9 1.2 %copy-done = bf16[1,128,4096]{2,1,0:T(8,128)(2,1)S(1)} copy-done((bf16[1,128,4096]{2,1,0:T(8,128)(2,1)S(1)}, bf16[1,128,4096]{2,1,0:T(8,128)(2,1)}, u32[]{:S(2)}) %copy-start) | copy-done | bytes 1048600
  12.2 3.3 %local_grad.1.local_ref = f32[128,4352]{1,0:T(8,128)S(1)} custom-call(f32[8]{0:T(128)S(1)} %copy-done.2, f32[8,4096]{1,0:T(8,128)S(1)} %copy-done.1, bf16[1,128,4096]{2,1,0:T(8,128)(2,1)S(1)} %copy-done), custom_call_target="tpu_custom_call" | custom-call | flops 1073741824 | bytes 3145728 | tf_op jit(solution)/shard_map/local_grad/pallas_call | solution.py:377
  15.5 2.0 %all-to-all-done = f32[16,48,128]{2,1,0:T(8,128)S(1)} async-done(((f32[16,48,128]{2,1,0:T(8,128)}), f32[16,48,128]{2,1,0:T(8,128)S(1)}, u32[]{:S(2)}, u32[]{:S(2)}) %all-to-all-start) | async-done | bytes 393248 | tf_op jit(solution)/shard_map/all_to_all | solution.py:314
  17.5 2.7 %collective-permute-start = (f32[10,8,128]{2,1,0:T(8,128)S(1)}, f32[10,8,128]{2,1,0:T(8,128)S(1)}, u32[]{:S(2)}, u32[]{:S(2)}) collective-permute-start(f32[10,8,128]{2,1,0:T(8,128)S(1)} %half.1.own_ref), channel_id=1, source_target_pairs={{0,4},{1,5},{2,6},{3,7},{4,0},{5,1},{6,2},{7,3},{8,12},{9,13},{10,... | collective-permute-start | bytes 122888 | tf_op jit(solution)/shard_map/ppermute | solution.py:404
  20.2 2.8 %collective-permute-done.other_ref = f32[10,8,128]{2,1,0:T(8,128)S(1)} collective-permute-done((f32[10,8,128]{2,1,0:T(8,128)S(1)}, f32[10,8,128]{2,1,0:T(8,128)S(1)}, u32[]{:S(2)}, u32[]{:S(2)}) %collective-permute-start) | collective-permute-done | bytes 40992 | tf_op jit(solution)/shard_map/ppermute | solution.py:404
  23.0 8.3 %all_to_all.10.back_ref = f32[16,24,128]{2,1,0:T(8,128)S(1)} all-to-all(f32[16,24,128]{2,1,0:T(8,128)S(1)} %scan.1), channel_id=1, replica_groups={{25,24,27,26,17,16,19,18,9,8,11,10,1,0,3,2},{29,28,31,30,21,20,23,22,13..., dimensions={0} | all-to-all | bytes 393216 | tf_op jit(solution)/shard_map/all_to_all | solution.py:314
  31.3 1.2 %finish.1 = (bf16[1,128,4096]{2,1,0:T(8,128)(2,1)}, f32[8,1024]{1,0:T(8,128)}) custom-call(f32[8,4096]{1,0:T(8,128)S(1)} %copy-done.1, f32[128,4352]{1,0:T(8,128)S(1)} %local_grad.1.local_ref, f32[16,24,128]{2,1,0:T(8,128)S(1)} %all_to_all.10.back_ref), custom_call_target="tpu_custom_call" | custom-call | tf_op jit(solution)/shard_map/finish/pallas_call | solution.py:414
  (2 shorter events, 0.1 us)
Async XLA Ops:
  0.6 10.3 %copy-start.2 = (f32[8]{0:T(128)S(1)}, f32[8]{0:T(128)}, u32[]{:S(2)}) copy-start(f32[8]{0:T(128)} %rates_hbm.3) | copy-start | bytes 100
  0.6 10.3 %copy-start.1 = (f32[8,4096]{1,0:T(8,128)S(1)}, f32[8,4096]{1,0:T(8,128)}, u32[]{:S(2)}) copy-start(f32[8,4096]{1,0:T(8,128)} %residues_ref.3) | copy-start | bytes 393220
  4.1 13.3 %all-to-all-start = ((f32[16,48,128]{2,1,0:T(8,128)}), f32[16,48,128]{2,1,0:T(8,128)S(1)}, u32[]{:S(2)}, u32[]{:S(2)}) async-start(f32[16,48,128]{2,1,0:T(8,128)} %bitcast.4), calls=%async_computation | async-start | bytes 786432 | tf_op jit(solution)/shard_map/all_to_all | solution.py:314
  10.9 1.2 %copy-start = (bf16[1,128,4096]{2,1,0:T(8,128)(2,1)S(1)}, bf16[1,128,4096]{2,1,0:T(8,128)(2,1)}, u32[]{:S(2)}) copy-start(bf16[1,128,4096]{2,1,0:T(8,128)(2,1)} %grad_hbm.3) | copy-start | bytes 3145732
  17.5 5.4 %collective-permute-start = (f32[10,8,128]{2,1,0:T(8,128)S(1)}, f32[10,8,128]{2,1,0:T(8,128)S(1)}, u32[]{:S(2)}, u32[]{:S(2)}) collective-permute-start(f32[10,8,128]{2,1,0:T(8,128)S(1)} %half.1.own_ref), channel_id=1, source_target_pairs={{0,4},{1,5},{2,6},{3,7},{4,0},{5,1},{6,2},{7,3},{8,12},{9,13},{10,... | collective-permute-start | bytes 122888 | tf_op jit(solution)/shard_map/ppermute | solution.py:404

commit v8 on v7

--- a/solution.py
+++ b/solution.py
@@ -181,6 +181,10 @@
     return local_ref[0:modes, last : last + width]
 
 
+def place(b, j, half):
+    return (b // 2 * half + j) * 2 + b % 2
+
+
 def steps(count, body, start):
     return lax.fori_loop(0, count, body, start, unroll=count <= 8)
 
@@ -196,13 +200,13 @@
         def sequence(b, total):
             def state(j, pair):
                 total, incoming = pair
-                at = ((b * half + half - 1 - j) ^ mask) * pieces + k
+                at = (place(b, half - 1 - j, half) ^ mask) * pieces + k
                 weights = terms_ref[at, modes : 2 * modes, :]
                 total = total + (terms_ref[at, 2 * modes : 3 * modes, :] + incoming * weights)
                 return total, terms_ref[at, 0:modes, :] + decay * incoming
 
             def weight(j, before):
-                return terms_ref[((b * half + j) ^ mask) * pieces + k, modes : 2 * modes, :] + decay * before
+                return terms_ref[(place(b, j, half) ^ mask) * pieces + k, modes : 2 * modes, :] + decay * before
 
             total, incoming = steps(half, state, (total, zero))
             out_ref[b * pieces + k] = jnp.where(later, incoming, steps(half, weight, zero))
@@ -225,7 +229,7 @@
             other = other_ref[b * pieces + k]
 
             def block(j, incoming):
-                at = (b * half + half - 1 - j) ^ mask
+                at = place(b, half - 1 - j, half) ^ mask
                 out_ref[at, k * modes : (k + 1) * modes, :] = incoming
                 return terms_ref[at * pieces + k, 0:modes, :] + decay * incoming
 
@@ -234,8 +238,9 @@
 
         totals.append(steps(batch_count, sequence, total))
     if paired:
-        for at in range(batch_count * half):
-            out_ref[at ^ mask, pieces * modes :, :] = totals[at // half // 2]
+        for b in range(batch_count):
+            for j in range(half):
+                out_ref[place(b, j, half) ^ mask, pieces * modes :, :] = totals[b // 2]
     else:
 
         def spread(at, carry):
@@ -306,11 +311,13 @@
     pieces = channels // (owners * width)
     anywhere = pl.BlockSpec(memory_space=pl.ANY)
     whole = pl.BlockSpec(memory_space=pltpu.VMEM)
-    mask = (batch_count - 1) * half + 1 if half > 1 and owners & (owners - 1) == 0 else 0
+    mask = place(batch_count - 1, 1, half) if half > 1 and owners & (owners - 1) == 0 else 0
 
     def exchange(slots):
-        places = [d * block_count + j for d in range(batch_count) for j in range(half)]
-        groups = [[first + places[p ^ mask] for p in range(owners)] for first in (0, half)]
+        where = {
+            place(d, j, half) ^ mask: d * block_count + j for d in range(batch_count) for j in range(half)
+        }
+        groups = [[first + where[p] for p in range(owners)] for first in (0, half)]
         return lax.all_to_all(slots, ("dp", "seq"), 0, 0, axis_index_groups=groups)
 
     slot_count = min(owners, chunks)

time: 32.8 us -> 32.6 us (level)
  no operation moved by 1% of the time
where the time goes in v8:
time: 32.6 us; the launch traced here: 32.3 us
  starting transfers between devices  9.46 us (29%)
  blocking collectives  8.22 us (25%)
  Pallas kernels  8.05 us (25%)
  waiting for transfers between devices  4.67 us (14%)
  local copies, waits for them, and re-layouts  1.23 us (4%)
  between operations  0.69 us (2%)
    all_to_all x1, blocking collectives, exchange(): return lax.all_to_all(slots, ('dp', 'seq'), 0, 0, axis_index_groups=groups)  8.22 us
    all_to_all x1, starting transfers between devices, exchange(): return lax.all_to_all(slots, ('dp', 'seq'), 0, 0, axis_index_groups=groups)  6.77 us
    pallas_call x1, Pallas kernels, local(): pl.pallas_call(functools.partial(terms_kernel, 2, 256, places), in_specs=...  3.48 us
    pallas_call x1, Pallas kernels, local(): pl.pallas_call(functools.partial(local_grad_kernel, 512), in_specs=[anywh...  3.3 us
    ppermute x1, waiting for transfers between devices, local(): lax.ppermute(cross, 'seq', [(s, (s + half) % block_count) for s in range(...  2.95 us
    ppermute x1, starting transfers between devices, local(): lax.ppermute(cross, 'seq', [(s, (s + half) % block_count) for s in range(...  2.68 us
    all_to_all x1, waiting for transfers between devices, exchange(): return lax.all_to_all(slots, ('dp', 'seq'), 0, 0, axis_index_groups=groups)  1.72 us
    unnamed x6, local copies, waits for them, and re-layouts  1.23 us
  transfers between devices with their start and end apart: 2, of which 2 were waited for; matrix products, arithmetic and copies ran while one was open for 0% of the time, Pallas kernels for 10%

profile of v8, /device:TPU:0, one launch (start us, length us, event | category | flops | bytes accessed | tf_op | source)
XLA Modules:
  0.0 32.3 jit_solution(7522662590943599012)
XLA Ops:
  0.6 0.0 copy-start.2
  0.6 0.0 copy-start.1
  0.7 3.5 %terms.1 = f32[16,2,24,128]{3,2,1,0:T(8,128)} custom-call(f32[8]{0:T(128)} %rates_hbm.3, bf16[1,128,4096]{2,1,0:T(8,128)(2,1)} %grad_hbm.3, bf16[1,128,4096]{2,1,0:T(8,128)(2,1)} %in_hbm.1), custom_call_target="tpu_custom_call" | custom-call | tf_op jit(solution)/shard_map/terms/pallas_call | solution.py:363
  4.1 6.8 %all-to-all-start = ((f32[16,48,128]{2,1,0:T(8,128)}), f32[16,48,128]{2,1,0:T(8,128)S(1)}, u32[]{:S(2)}, u32[]{:S(2)}) async-start(f32[16,48,128]{2,1,0:T(8,128)} %bitcast.4), calls=%async_computation | async-start | bytes 786432 | tf_op jit(solution)/shard_map/all_to_all | solution.py:321
  10.9 0.0 copy-done.2
  10.9 0.0 copy-done.1
  10.9 0.0 copy-start
  10.9 1.2 %copy-done = bf16[1,128,4096]{2,1,0:T(8,128)(2,1)S(1)} copy-done((bf16[1,128,4096]{2,1,0:T(8,128)(2,1)S(1)}, bf16[1,128,4096]{2,1,0:T(8,128)(2,1)}, u32[]{:S(2)}) %copy-start) | copy-done | bytes 1048600
  12.2 3.3 %local_grad.1.local_ref = f32[128,4352]{1,0:T(8,128)S(1)} custom-call(f32[8]{0:T(128)S(1)} %copy-done.2, f32[8,4096]{1,0:T(8,128)S(1)} %copy-done.1, bf16[1,128,4096]{2,1,0:T(8,128)(2,1)S(1)} %copy-done), custom_call_target="tpu_custom_call" | custom-call | flops 1073741824 | bytes 3145728 | tf_op jit(solution)/shard_map/local_grad/pallas_call | solution.py:384
  15.5 1.7 %all-to-all-done = f32[16,48,128]{2,1,0:T(8,128)S(1)} async-done(((f32[16,48,128]{2,1,0:T(8,128)}), f32[16,48,128]{2,1,0:T(8,128)S(1)}, u32[]{:S(2)}, u32[]{:S(2)}) %all-to-all-start) | async-done | bytes 393248 | tf_op jit(solution)/shard_map/all_to_all | solution.py:321
  17.2 2.7 %collective-permute-start = (f32[10,8,128]{2,1,0:T(8,128)S(1)}, f32[10,8,128]{2,1,0:T(8,128)S(1)}, u32[]{:S(2)}, u32[]{:S(2)}) collective-permute-start(f32[10,8,128]{2,1,0:T(8,128)S(1)} %half.1.own_ref), channel_id=1, source_target_pairs={{0,4},{1,5},{2,6},{3,7},{4,0},{5,1},{6,2},{7,3},{8,12},{9,13},{10,... | collective-permute-start | bytes 122888 | tf_op jit(solution)/shard_map/ppermute | solution.py:411
  19.9 3.0 %collective-permute-done.other_ref = f32[10,8,128]{2,1,0:T(8,128)S(1)} collective-permute-done((f32[10,8,128]{2,1,0:T(8,128)S(1)}, f32[10,8,128]{2,1,0:T(8,128)S(1)}, u32[]{:S(2)}, u32[]{:S(2)}) %collective-permute-start) | collective-permute-done | bytes 40992 | tf_op jit(solution)/shard_map/ppermute | solution.py:411
  22.9 8.2 %all_to_all.10.back_ref = f32[16,24,128]{2,1,0:T(8,128)S(1)} all-to-all(f32[16,24,128]{2,1,0:T(8,128)S(1)} %scan.1), channel_id=1, replica_groups={{25,17,24,16,27,19,26,18,9,1,8,0,11,3,10,2},{29,21,28,20,31,23,30,22,13..., dimensions={0} | all-to-all | bytes 393216 | tf_op jit(solution)/shard_map/all_to_all | solution.py:321
  31.1 1.2 %finish.1 = (bf16[1,128,4096]{2,1,0:T(8,128)(2,1)}, f32[8,1024]{1,0:T(8,128)}) custom-call(f32[8,4096]{1,0:T(8,128)S(1)} %copy-done.1, f32[128,4352]{1,0:T(8,128)S(1)} %local_grad.1.local_ref, f32[16,24,128]{2,1,0:T(8,128)S(1)} %all_to_all.10.back_ref), custom_call_target="tpu_custom_call" | custom-call | tf_op jit(solution)/shard_map/finish/pallas_call | solution.py:421
  (2 shorter events, 0.1 us)
Async XLA Ops:
  0.6 10.3 %copy-start.2 = (f32[8]{0:T(128)S(1)}, f32[8]{0:T(128)}, u32[]{:S(2)}) copy-start(f32[8]{0:T(128)} %rates_hbm.3) | copy-start | bytes 100
  0.6 10.3 %copy-start.1 = (f32[8,4096]{1,0:T(8,128)S(1)}, f32[8,4096]{1,0:T(8,128)}, u32[]{:S(2)}) copy-start(f32[8,4096]{1,0:T(8,128)} %residues_ref.3) | copy-start | bytes 393220
  4.1 13.0 %all-to-all-start = ((f32[16,48,128]{2,1,0:T(8,128)}), f32[16,48,128]{2,1,0:T(8,128)S(1)}, u32[]{:S(2)}, u32[]{:S(2)}) async-start(f32[16,48,128]{2,1,0:T(8,128)} %bitcast.4), calls=%async_computation | async-start | bytes 786432 | tf_op jit(solution)/shard_map/all_to_all | solution.py:321
  10.9 1.2 %copy-start = (bf16[1,128,4096]{2,1,0:T(8,128)(2,1)S(1)}, bf16[1,128,4096]{2,1,0:T(8,128)(2,1)}, u32[]{:S(2)}) copy-start(bf16[1,128,4096]{2,1,0:T(8,128)(2,1)} %grad_hbm.3) | copy-start | bytes 3145732
  17.2 5.6 %collective-permute-start = (f32[10,8,128]{2,1,0:T(8,128)S(1)}, f32[10,8,128]{2,1,0:T(8,128)S(1)}, u32[]{:S(2)}, u32[]{:S(2)}) collective-permute-start(f32[10,8,128]{2,1,0:T(8,128)S(1)} %half.1.own_ref), channel_id=1, source_target_pairs={{0,4},{1,5},{2,6},{3,7},{4,0},{5,1},{6,2},{7,3},{8,12},{9,13},{10,... | collective-permute-start | bytes 122888 | tf_op jit(solution)/shard_map/ppermute | solution.py:411

commit v9 on v8

--- a/solution.py
+++ b/solution.py
@@ -108,16 +108,7 @@
             part = slice(first, first + sub)
             grad = grad_ref[:, part]
             block = in_ref[:, part]
-            twice = jnp.concatenate([block, block], axis=0)
-            sums = jnp.dot(before_ref[...], twice, preferred_element_type=jnp.float32)
-            twice = jnp.concatenate([grad, grad], axis=0)
-            states = jnp.dot(after_ref[...], twice, preferred_element_type=jnp.float32)
-            last = slice((groups - 1) * modes, groups * modes)
-            carry, state = sums[last], states[last]
-            local = sums[0:modes] * states[0:modes]
-            for u in range(1, groups - 1):
-                at = slice(u * modes, (u + 1) * modes)
-                local = local + sums[at] * states[at]
+            near = jnp.zeros((modes, sub), jnp.float32)
             grad32 = grad.astype(jnp.float32).reshape(rows // SUBLANES, SUBLANES, sub)
             block32 = block.astype(jnp.float32).reshape(rows // SUBLANES, SUBLANES, sub)
             for k in range(GROUP):
@@ -126,7 +117,19 @@
                 if k:
                     product = jnp.where(in_group + k < GROUP, product, 0.0)
                 weight = jnp.concatenate([lag_ref[k]] * (sub // LANES), axis=1)
-                local = local + weight * jnp.sum(product, axis=0, keepdims=True)
+                near = near + weight * jnp.sum(product, axis=0, keepdims=True)
+            twice = jnp.concatenate([block, block], axis=0)
+            sums = jnp.dot(before_ref[...], twice, preferred_element_type=jnp.float32)
+            twice = jnp.concatenate([grad, grad], axis=0)
+            states = jnp.dot(after_ref[...], twice, preferred_element_type=jnp.float32)
+            last = slice((groups - 1) * modes, groups * modes)
+            carry, state = sums[last], states[last]
+            lines = [None] * 4
+            for u in range(groups - 1):
+                at = slice(u * modes, (u + 1) * modes)
+                product = sums[at] * states[at]
+                lines[u % 4] = product if u < 4 else lines[u % 4] + product
+            local = sum(lines, near)
             for k in range(sub // LANES):
                 for low, high, at in places(first // LANES + k):
                     lanes = slice(k * LANES + low, k * LANES + high)

time: 32.6 us -> 32.7 us (level)
  no operation moved by 1% of the time
where the time goes in v9:
time: 32.7 us; the launch traced here: 32.3 us
  starting transfers between devices  9.45 us (29%)
  blocking collectives  8.22 us (25%)
  Pallas kernels  8.07 us (25%)
  waiting for transfers between devices  4.68 us (14%)
  local copies, waits for them, and re-layouts  1.23 us (4%)
  between operations  0.69 us (2%)
    all_to_all x1, blocking collectives, exchange(): return lax.all_to_all(slots, ('dp', 'seq'), 0, 0, axis_index_groups=groups)  8.22 us
    all_to_all x1, starting transfers between devices, exchange(): return lax.all_to_all(slots, ('dp', 'seq'), 0, 0, axis_index_groups=groups)  6.78 us
    pallas_call x1, Pallas kernels, local(): pl.pallas_call(functools.partial(terms_kernel, 2, 256, places), in_specs=...  3.5 us
    pallas_call x1, Pallas kernels, local(): pl.pallas_call(functools.partial(local_grad_kernel, 512), in_specs=[anywh...  3.3 us
    ppermute x1, waiting for transfers between devices, local(): lax.ppermute(cross, 'seq', [(s, (s + half) % block_count) for s in range(...  2.96 us
    ppermute x1, starting transfers between devices, local(): lax.ppermute(cross, 'seq', [(s, (s + half) % block_count) for s in range(...  2.67 us
    all_to_all x1, waiting for transfers between devices, exchange(): return lax.all_to_all(slots, ('dp', 'seq'), 0, 0, axis_index_groups=groups)  1.72 us
    unnamed x6, local copies, waits for them, and re-layouts  1.23 us
  transfers between devices with their start and end apart: 2, of which 2 were waited for; matrix products, arithmetic and copies ran while one was open for 0% of the time, Pallas kernels for 10%

profile of v9, /device:TPU:0, one launch (start us, length us, event | category | flops | bytes accessed | tf_op | source)
XLA Modules:
  0.0 32.3 jit_solution(4812835731985094801)
XLA Ops:
  0.6 0.0 copy-start.2
  0.6 0.0 copy-start.1
  0.7 3.5 %terms.1 = f32[16,2,24,128]{3,2,1,0:T(8,128)} custom-call(f32[8]{0:T(128)} %rates_hbm.3, bf16[1,128,4096]{2,1,0:T(8,128)(2,1)} %grad_hbm.3, bf16[1,128,4096]{2,1,0:T(8,128)(2,1)} %in_hbm.1), custom_call_target="tpu_custom_call" | custom-call | tf_op jit(solution)/shard_map/terms/pallas_call | solution.py:366
  4.2 6.8 %all-to-all-start = ((f32[16,48,128]{2,1,0:T(8,128)}), f32[16,48,128]{2,1,0:T(8,128)S(1)}, u32[]{:S(2)}, u32[]{:S(2)}) async-start(f32[16,48,128]{2,1,0:T(8,128)} %bitcast.4), calls=%async_computation | async-start | bytes 786432 | tf_op jit(solution)/shard_map/all_to_all | solution.py:324
  10.9 0.0 copy-done.2
  10.9 0.0 copy-done.1
  11.0 0.0 copy-start
  11.0 1.2 %copy-done = bf16[1,128,4096]{2,1,0:T(8,128)(2,1)S(1)} copy-done((bf16[1,128,4096]{2,1,0:T(8,128)(2,1)S(1)}, bf16[1,128,4096]{2,1,0:T(8,128)(2,1)}, u32[]{:S(2)}) %copy-start) | copy-done | bytes 1048600
  12.2 3.3 %local_grad.1.local_ref = f32[128,4352]{1,0:T(8,128)S(1)} custom-call(f32[8]{0:T(128)S(1)} %copy-done.2, f32[8,4096]{1,0:T(8,128)S(1)} %copy-done.1, bf16[1,128,4096]{2,1,0:T(8,128)(2,1)S(1)} %copy-done), custom_call_target="tpu_custom_call" | custom-call | flops 1073741824 | bytes 3145728 | tf_op jit(solution)/shard_map/local_grad/pallas_call | solution.py:387
  15.5 1.7 %all-to-all-done = f32[16,48,128]{2,1,0:T(8,128)S(1)} async-done(((f32[16,48,128]{2,1,0:T(8,128)}), f32[16,48,128]{2,1,0:T(8,128)S(1)}, u32[]{:S(2)}, u32[]{:S(2)}) %all-to-all-start) | async-done | bytes 393248 | tf_op jit(solution)/shard_map/all_to_all | solution.py:324
  17.2 2.7 %collective-permute-start = (f32[10,8,128]{2,1,0:T(8,128)S(1)}, f32[10,8,128]{2,1,0:T(8,128)S(1)}, u32[]{:S(2)}, u32[]{:S(2)}) collective-permute-start(f32[10,8,128]{2,1,0:T(8,128)S(1)} %half.1.own_ref), channel_id=1, source_target_pairs={{0,4},{1,5},{2,6},{3,7},{4,0},{5,1},{6,2},{7,3},{8,12},{9,13},{10,... | collective-permute-start | bytes 122888 | tf_op jit(solution)/shard_map/ppermute | solution.py:414
  19.9 3.0 %collective-permute-done.other_ref = f32[10,8,128]{2,1,0:T(8,128)S(1)} collective-permute-done((f32[10,8,128]{2,1,0:T(8,128)S(1)}, f32[10,8,128]{2,1,0:T(8,128)S(1)}, u32[]{:S(2)}, u32[]{:S(2)}) %collective-permute-start) | collective-permute-done | bytes 40992 | tf_op jit(solution)/shard_map/ppermute | solution.py:414
  22.9 8.2 %all_to_all.10.back_ref = f32[16,24,128]{2,1,0:T(8,128)S(1)} all-to-all(f32[16,24,128]{2,1,0:T(8,128)S(1)} %scan.1), channel_id=1, replica_groups={{25,17,24,16,27,19,26,18,9,1,8,0,11,3,10,2},{29,21,28,20,31,23,30,22,13..., dimensions={0} | all-to-all | bytes 393216 | tf_op jit(solution)/shard_map/all_to_all | solution.py:324
  31.1 1.2 %finish.1 = (bf16[1,128,4096]{2,1,0:T(8,128)(2,1)}, f32[8,1024]{1,0:T(8,128)}) custom-call(f32[8,4096]{1,0:T(8,128)S(1)} %copy-done.1, f32[128,4352]{1,0:T(8,128)S(1)} %local_grad.1.local_ref, f32[16,24,128]{2,1,0:T(8,128)S(1)} %all_to_all.10.back_ref), custom_call_target="tpu_custom_call" | custom-call | tf_op jit(solution)/shard_map/finish/pallas_call | solution.py:424
  (2 shorter events, 0.1 us)
Async XLA Ops:
  0.6 10.3 %copy-start.2 = (f32[8]{0:T(128)S(1)}, f32[8]{0:T(128)}, u32[]{:S(2)}) copy-start(f32[8]{0:T(128)} %rates_hbm.3) | copy-start | bytes 100
  0.6 10.3 %copy-start.1 = (f32[8,4096]{1,0:T(8,128)S(1)}, f32[8,4096]{1,0:T(8,128)}, u32[]{:S(2)}) copy-start(f32[8,4096]{1,0:T(8,128)} %residues_ref.3) | copy-start | bytes 393220
  4.2 13.0 %all-to-all-start = ((f32[16,48,128]{2,1,0:T(8,128)}), f32[16,48,128]{2,1,0:T(8,128)S(1)}, u32[]{:S(2)}, u32[]{:S(2)}) async-start(f32[16,48,128]{2,1,0:T(8,128)} %bitcast.4), calls=%async_computation | async-start | bytes 786432 | tf_op jit(solution)/shard_map/all_to_all | solution.py:324
  11.0 1.2 %copy-start = (bf16[1,128,4096]{2,1,0:T(8,128)(2,1)S(1)}, bf16[1,128,4096]{2,1,0:T(8,128)(2,1)}, u32[]{:S(2)}) copy-start(bf16[1,128,4096]{2,1,0:T(8,128)(2,1)} %grad_hbm.3) | copy-start | bytes 3145732
  17.2 5.6 %collective-permute-start = (f32[10,8,128]{2,1,0:T(8,128)S(1)}, f32[10,8,128]{2,1,0:T(8,128)S(1)}, u32[]{:S(2)}, u32[]{:S(2)}) collective-permute-start(f32[10,8,128]{2,1,0:T(8,128)S(1)} %half.1.own_ref), channel_id=1, source_target_pairs={{0,4},{1,5},{2,6},{3,7},{4,0},{5,1},{6,2},{7,3},{8,12},{9,13},{10,... | collective-permute-start | bytes 122888 | tf_op jit(solution)/shard_map/ppermute | solution.py:414
